TPU v7x, 256 devices: a whole 4x4x8 slice. The times are simulated.
256 devices in a mesh: ctx: 16 (over z, core), head: 16 (over y, x).
Axes of the slice: x: 4, y: 4, z: 8, core: 2. Of those that a mesh axis runs over, the one named last changes fastest.
Arguments:
- inputs: bfloat16 [16384, 8192], P('ctx', 'head'), may hold values from -6 to 6
- upstream: bfloat16 [16384, 8192], P('ctx', 'head'), may hold values from -1.1953125 to 1.1953125
- step_size: float32 [16384, 128], P('ctx', 'head'), may hold values from 0 to 0.5, as said below
- decay_rate: float32 [128], P('head'), may hold values from 0 to 0.16, as said below
- write_proj: bfloat16 [16384, 1024], P('ctx'), may hold values from -2.390625 to 2.390625
- read_proj: bfloat16 [16384, 1024], P('ctx'), may hold values from -2.390625 to 2.390625
- init_state: float32 [128, 64, 128], P('head'), may hold values from -6 to 6
- skip_gain: float32 [128], P('head'), may hold values from 0.5 to 2
Outputs:
- grad_inputs: bfloat16 [16384, 8192], P(('ctx', 'head'))
- grad_write: bfloat16 [16384, 1024], P(('ctx', 'head'))
- grad_read: bfloat16 [16384, 1024], P(('ctx', 'head'))
Inputs may be any that keep to these rules, and one draw needn't show every extreme that they name: `step_size`: positive step sizes. `decay_rate`: positive decay rates.
All inputs are finite; a program needn't handle non-finite values.
Results may differ from a plain program's by a relative error of at most 0.0024.
Values may be sent and summed in bfloat16 or wider, within the bound.
No kernel may reach another device: no remote copies, remote signals or barrier semaphores. Data moves between devices by JAX's collectives and lax.ppermute only.
A program may use at most 64 MiB of HBM per device.

v0:
```python
import jax
import jax.numpy as jnp
from jax import lax
from jax.sharding import PartitionSpec as P

HEADS = 128
HEAD_SIZE = 64
STATE = 128
GROUPS = 8
BLOCK = 256


highest = lax.Precision.HIGHEST


def prefix(part, axis, combine, identity, reverse):
    count = lax.axis_size(axis)
    place = lax.axis_index(axis)
    ahead = count - 1 - place if reverse else place
    gathered = jax.tree.map(lambda a: lax.all_gather(a, axis), part)
    state = jax.tree.map(lambda a, e: jnp.zeros_like(a) + jnp.asarray(e, a.dtype), part, identity)

    def one(hop, state):
        source = count - 1 - hop if reverse else hop
        return combine(
            state, jax.tree.map(lambda a: lax.dynamic_index_in_dim(a, source, 0, False), gathered)
        )

    return lax.fori_loop(0, ahead, one, state)


def decay_matrix(cum_log):
    length = cum_log.shape[0]
    lower = (jnp.arange(length)[:, None] >= jnp.arange(length)[None, :])[None, :, :]
    spread = cum_log.T[:, :, None] - cum_log.T[:, None, :]
    return jnp.where(lower, jnp.exp(jnp.where(lower, spread, 0.0)), 0.0)


def block_sums(inputs, upstream, steps, writes, reads, cum_log):
    last_log = cum_log[-1]
    weight_in = jnp.exp(last_log[None, :] - cum_log) * steps
    weight_back = jnp.exp(cum_log)
    into = jnp.einsum("thp,thn->hpn", weight_in[:, :, None] * inputs, writes, precision=highest)
    back = jnp.einsum("thp,thn->hpn", weight_back[:, :, None] * upstream, reads, precision=highest)
    return (into, back)


def block_grads(
    inputs,
    upstream,
    products,
    steps,
    writes,
    reads,
    pair_dots,
    cum_log,
    skip,
    state_in,
    adjoint_out,
):
    decays = decay_matrix(cum_log)
    last_log = cum_log[-1]
    kernel = products * decays
    weighted = kernel * steps.T[:, None, :]
    grad_read = jnp.exp(cum_log)[:, :, None] * jnp.einsum(
        "thp,hpn->thn", upstream, state_in, precision=highest
    )
    grad_read = grad_read + jnp.einsum("hts,shn->thn", weighted, writes, precision=highest)
    remain = jnp.exp(last_log[None, :] - cum_log)[:, :, None]
    coupled = pair_dots * jnp.swapaxes(decays, 1, 2)
    through = jnp.einsum("htu,uhp->thp", coupled, upstream, precision=highest)
    through = through + remain * jnp.einsum("hpn,thn->thp", adjoint_out, writes, precision=highest)
    grad_input = steps[:, :, None] * through + skip[None, :, None] * upstream
    flipped = jnp.swapaxes(kernel, 1, 2)
    grad_write = jnp.einsum("htu,uhn->thn", flipped, reads, precision=highest)
    grad_write = grad_write + remain * jnp.einsum(
        "thp,hpn->thn", inputs, adjoint_out, precision=highest
    )
    return (grad_input, steps[:, :, None] * grad_write, grad_read)


def per_device(
    inputs, upstream, step_size, decay_rate, write_proj, read_proj, init_state, skip_gain
):
    length = inputs.shape[0]
    heads_dev = step_size.shape[1]
    per_group = HEADS // GROUPS
    within = min(heads_dev, per_group)
    spanned = max(1, heads_dev // per_group)
    sources = per_group // within
    blocks = length // BLOCK
    column = lax.axis_index("head") * heads_dev // per_group * STATE
    own_write = lax.dynamic_slice_in_dim(write_proj, column, spanned * STATE, 1)
    own_read = lax.dynamic_slice_in_dim(read_proj, column, spanned * STATE, 1)
    shaped = (
        inputs.reshape(blocks, BLOCK, heads_dev, HEAD_SIZE),
        upstream.reshape(blocks, BLOCK, heads_dev, HEAD_SIZE),
        step_size.reshape(blocks, BLOCK, heads_dev),
        own_write.reshape(blocks, BLOCK, spanned, STATE),
        own_read.reshape(blocks, BLOCK, spanned, STATE),
    )

    def summarize(raw):
        ins, ups, steps, wr_grp, rd_grp = raw
        cum_log = jnp.cumsum(-steps * decay_rate[None, :], axis=0)
        writes = jnp.repeat(wr_grp.astype(jnp.float32), within, axis=1)
        reads = jnp.repeat(rd_grp.astype(jnp.float32), within, axis=1)
        into, back = block_sums(
            ins.astype(jnp.float32), ups.astype(jnp.float32), steps, writes, reads, cum_log
        )
        return (cum_log, into, back)

    cum_logs, intos, backs = lax.map(summarize, shaped)
    last_logs = cum_logs[:, -1, :]
    running = jnp.cumsum(last_logs, axis=0)
    dev_log = running[-1]
    after = dev_log[None, :] - running
    before = running - last_logs
    dev_write = jnp.einsum("kh,khpn->hpn", jnp.exp(after), intos, precision=highest)
    dev_read = jnp.einsum("kh,khpn->hpn", jnp.exp(before), backs, precision=highest)
    decay = jnp.exp(dev_log)

    def combine(earlier, later):
        return (earlier[0] * later[0], later[0][:, None, None] * earlier[1] + later[1])

    neutral = (jnp.ones_like(decay), jnp.zeros_like(dev_write))
    pre_decay, pre_state = prefix((decay, dev_write), "ctx", combine, neutral, False)
    state_dev = pre_decay[:, None, None] * init_state + pre_state
    _, adjoint_dev = prefix((decay, dev_read), "ctx", combine, neutral, True)

    def forward_step(state, pack):
        last_log, into = pack
        return (jnp.exp(last_log)[:, None, None] * state + into, state)

    _, states_in = lax.scan(forward_step, state_dev, (last_logs, intos))

    def backward_step(adjoint, pack):
        last_log, back = pack
        return (jnp.exp(last_log)[:, None, None] * adjoint + back, adjoint)

    _, adjoints_out = lax.scan(backward_step, adjoint_dev, (last_logs, backs), reverse=True)

    def finish(pack):
        raw, cum_log, state_in, adjoint_out = pack
        ins, ups, steps, wr_grp, rd_grp = raw
        dots = jnp.einsum("tgn,ugn->gtu", wr_grp, rd_grp, preferred_element_type=jnp.float32)
        products = jnp.einsum("thp,shp->hts", ups, ins, preferred_element_type=jnp.float32)
        writes = jnp.repeat(wr_grp.astype(jnp.float32), within, axis=1)
        reads = jnp.repeat(rd_grp.astype(jnp.float32), within, axis=1)
        dots = jnp.repeat(dots, within, axis=0)
        grad_input, grad_write, grad_read = block_grads(
            ins.astype(jnp.float32),
            ups.astype(jnp.float32),
            products,
            steps,
            writes,
            reads,
            dots,
            cum_log,
            skip_gain,
            state_in,
            adjoint_out,
        )
        rows_input = grad_input.reshape(BLOCK, heads_dev * HEAD_SIZE).astype(jnp.bfloat16)
        part_write = jnp.sum(grad_write.reshape(BLOCK, spanned, within, STATE), axis=2)
        part_read = jnp.sum(grad_read.reshape(BLOCK, spanned, within, STATE), axis=2)
        part_write = part_write.astype(jnp.bfloat16).reshape(BLOCK, spanned * STATE)
        part_read = part_read.astype(jnp.bfloat16).reshape(BLOCK, spanned * STATE)
        return jnp.concatenate([rows_input, part_write, part_read], axis=1)

    rows = lax.map(finish, (shaped, cum_logs, states_in, adjoints_out))
    payload = rows.shape[-1]
    rows = rows.reshape(length, payload)
    moved = lax.all_to_all(rows, "head", split_axis=0, concat_axis=1, tiled=True)
    peers = lax.axis_size("head")
    share = moved.shape[0]
    pieces = moved.reshape(share, peers, payload)
    feature_cols = heads_dev * HEAD_SIZE
    grad_inputs = pieces[:, :, :feature_cols].reshape(share, HEADS * HEAD_SIZE)
    write_slots = pieces[:, :, feature_cols : feature_cols + spanned * STATE].astype(jnp.float32)
    read_slots = pieces[:, :, feature_cols + spanned * STATE :].astype(jnp.float32)
    grad_write = jnp.sum(write_slots.reshape(share, GROUPS, sources, STATE), axis=2)
    grad_read = jnp.sum(read_slots.reshape(share, GROUPS, sources, STATE), axis=2)
    grad_write = grad_write.astype(jnp.bfloat16).reshape(share, GROUPS * STATE)
    grad_read = grad_read.astype(jnp.bfloat16).reshape(share, GROUPS * STATE)
    return (grad_inputs, grad_write, grad_read)


def solution(mesh):
    placed = (
        P("ctx", "head"),
        P("ctx", "head"),
        P("ctx", "head"),
        P("head"),
        P("ctx", None),
        P("ctx", None),
        P("head", None, None),
        P("head"),
    )
    return jax.shard_map(
        per_device,
        mesh=mesh,
        in_specs=placed,
        out_specs=(P(("ctx", "head"), None), P(("ctx", "head"), None), P(("ctx", "head"), None)),
        check_vma=False,
    )
```

profile of v0, /device:TPU:1, one launch (start us, length us, event | category | flops | bytes accessed | tf_op | source)
XLA Modules:
  0.0 245.0 jit_solution(8564761616328662609)
XLA Ops:
  7.2 2.8 %reshape.220 = bf16[4,256,8,64]{3,2,1,0:T(8,128)(2,1)S(1)} reshape(bf16[1024,512]{1,0:T(8,128)(2,1)} %param.20) | data formatting | bytes 2097152 | tf_op jit(solution)/shard_map/reshape | solution.py:96
  10.0 1.9 copy.71
  12.0 2.8 %reshape.219 = bf16[4,256,8,64]{3,2,1,0:T(8,128)(2,1)S(1)} reshape(bf16[1024,512]{1,0:T(8,128)(2,1)} %param.21) | data formatting | bytes 2097152 | tf_op jit(solution)/shard_map/reshape | solution.py:97
  16.0 1.9 constant_dynamic-slice_fusion.4
  18.1 17.7 %while.78 = (s32[]{:T(128)}, f32[4,256,8]{1,2,0:T(8,128)S(1)}, f32[4,8,64,128]{3,2,1,0:T(8,128)S(1)}, f32[4,8,64,128]{3,2,1,0:T(8,128)S(1)}, f32[4,256,8]{1,2,0:...) while((s32[]{:T(128)}, f32[4,256,8]{1,2,0:T(8,128)S(1)}, ...), condition=%wide.region_3.4_spmd, body=%wide.region_0.3_spmd.sunk | while | flops 403515424 | bytes 1822445 | solution.py:113
  36.1 3.1 %fusion.83 = f32[8,1,64,128]{3,1,2,0:T(1,128)} fusion(f32[4,8,1,1]{0,2,3,1:T(1,128)S(1)} %copy.90, f32[4,8,64,128]{3,2,1,0:T(8,128)S(1)} %get-tuple-element.1026), kind=kOutput, calls=%fused_computation.117 | convolution fusion | flops 3145728 | bytes 1310848 | tf_op jit(solution)/shard_map/kh,khpn->hpn/dot_general | solution.py:119
  39.4 3.1 %fusion.85 = f32[8,1,64,128]{3,1,2,0:T(1,128)} fusion(f32[4,8,1,1]{0,2,3,1:T(1,128)S(1)} %copy.87, f32[4,8,64,128]{3,2,1,0:T(8,128)S(1)} %get-tuple-element.978), kind=kOutput, calls=%fused_computation.119 | convolution fusion | flops 3145728 | bytes 1310848 | tf_op jit(solution)/shard_map/kh,khpn->hpn/dot_general | solution.py:120
  42.5 21.2 %all-gather.2 = f32[16,1,8]{2,1,0:T(1,128)S(1)} all-gather(f32[1,1,8]{2,1,0:T(1,128)S(1)} %get-tuple-element.622), channel_id=1, replica_groups=mesh['ctx'=16,'head'=16] {'ctx'}, dimensions={0}, use_global_device_ids=true | all-gather | bytes 544 | tf_op jit(solution)/shard_map/all_gather | solution.py:20
  63.7 22.1 %all-gather.8.cloned.1.call-done = f32[128,64,128]{2,1,0:T(8,128)} async-done(((f32[8,64,128]{2,1,0:T(8,128)}), f32[128,64,128]{2,1,0:T(8,128)}) %all-gather.8.cloned.1.call-update) | async-done | bytes 4194320 | tf_op jit(solution)/shard_map/all_gather | solution.py:20
  89.1 3.5 %while.82 = (s32[]{:T(128)}, f32[8,64,128]{2,1,0:T(8,128)S(1)}, f32[4,8,64,128]{3,2,1,0:T(8,128)}, f32[4,8]{1,0:T(4,128)S(1)}, f32[4,8,64,128]{3,2,1,0:T(8,128)S(1)}, /*index=5*/s32[]{:T(128)}) while((s32[]{:T(128)}, f32[8,64,128]{2,1,0:T(8,128)S(1)}, f32[4,8,64,128]{3,2,1,0:T(8,128)}, f32[4,8]{1,0:T(4,128)S(1)}, ...), condition=%wide.region_8.9_spmd, body=%wide.region_7.8_spmd.sunk | while | flops 131074 | bytes 1311405 | solution.py:135
  92.6 36.2 %all-gather.6.cloned.1.call-done = f32[128,64,128]{2,1,0:T(8,128)} async-done(((f32[8,64,128]{2,1,0:T(8,128)}), f32[128,64,128]{2,1,0:T(8,128)}) %all-gather.6.cloned.1.call-update) | async-done | bytes 4194320 | tf_op jit(solution)/shard_map/all_gather | solution.py:20
  128.8 15.7 %while.79 = (s32[]{:T(128)}, f32[8,64,128]{2,1,0:T(8,128)S(1)}, s32[]{:T(128)}, f32[16,8]{1,0:T(8,128)S(1)}, f32[16,8,64,128]{3,2,1,0:T(8,128)}, /*index=5*/s32[]{:T(128)}, s32[]{:T(128)}, s32[]{:T(128)}, s32[]{:T(128)}) while((s32[]{:T(128)}, f32[8,64,128]{2,1,0:T(8,128)S(1)}, s32[]{:T(128)}, f32[16,8]{1,0:T(8,128)S(1)}, ...), condition=%wide.region_10.11_spmd, body=%wide.region_9.10_spmd.sunk | while | flops 131078 | bytes 786675 | solution.py:29
  145.6 3.5 %while.80 = (s32[]{:T(128)}, f32[8,64,128]{2,1,0:T(8,128)S(1)}, f32[4,8,64,128]{3,2,1,0:T(8,128)}, f32[4,8]{1,0:T(4,128)S(1)}, f32[4,8,64,128]{3,2,1,0:T(8,128)S(1)}, /*index=5*/s32[]{:T(128)}, s32[]{:T(128)}) while((s32[]{:T(128)}, f32[8,64,128]{2,1,0:T(8,128)S(1)}, f32[4,8,64,128]{3,2,1,0:T(8,128)}, f32[4,8]{1,0:T(4,128)S(1)}, ...), condition=%wide.region_12.13_spmd, body=%wide.region_11.12_spmd.sunk | while | flops 131075 | bytes 1310917 | solution.py:141
  149.2 58.5 %while.83 = (s32[]{:T(128)}, bf16[4,256,768]{2,1,0:T(8,128)(2,1)}, f32[4,256,8]{1,2,0:T(8,128)S(1)}, bf16[4,256,8,64]{1,3,2,0:T(8,128)(2,1)}, bf16[4,256,1,128]{...) while((s32[]{:T(128)}, bf16[4,256,768]{2,1,0:T(8,128)(2,1)}, ...), condition=%wide.region_16.17_spmd, body=%wide.region_13.16_spmd.sunk | while | flops 2709915648 | bytes 23221060 | solution.py:171
  151.2 1.8 select_multiply_fusion.2
  157.0 2.2 fusion.154
  165.8 1.8 select_multiply_fusion.2
  171.7 2.2 fusion.154
  180.4 1.8 select_multiply_fusion.2
  186.3 2.2 fusion.154
  195.1 1.8 select_multiply_fusion.2
  200.9 2.2 fusion.154
  203.3 1.7 fusion.158
  207.7 27.9 %all_to_all.16 = bf16[16,64,768]{2,1,0:T(8,128)(2,1)S(1)} all-to-all(bf16[16,64,768]{2,1,0:T(8,128)(2,1)} %bitcast.60), channel_id=1, replica_groups=mesh['ctx'=16,'head'=16] {'head'}, dimensions={0} | all-to-all | bytes 3145728 | tf_op jit(solution)/shard_map/all_to_all | solution.py:174
  (220 shorter events, 89.9 us)
Async XLA Ops:
  7.2 78.6 %all-gather.8.cloned.1.call-start = ((), (), s32[]{:S(2)}) async-start(), calls=%async_computation.2 | async-start | bytes 4456448 | tf_op jit(solution)/shard_map/all_gather | solution.py:20
  15.9 2.2 copy-start.2
  16.0 2.2 copy-start.4
  35.8 50.0 %copy-start = (bf16[4,256,8,64]{1,3,2,0:T(8,128)(2,1)}, bf16[4,256,8,64]{1,3,2,0:T(8,128)(2,1)S(1)}, u32[]{:S(2)}) copy-start(bf16[4,256,8,64]{1,3,2,0:T(8,128)(2,1)S(1)} %get-tuple-element.1084) | copy-start | bytes 3145732
  39.2 89.5 %all-gather.6.cloned.1.call-start = ((), (), s32[]{:S(2)}) async-start(), calls=%async_computation.1 | async-start | bytes 4456448 | tf_op jit(solution)/shard_map/all_gather | solution.py:20
  145.6 3.5 %copy-start.3 = (f32[8]{0:T(128)S(1)}, f32[8]{0:T(128)}, u32[]{:S(2)}) copy-start(f32[8]{0:T(128)} %param.27) | copy-start | bytes 100
  157.0 2.4 copy-start.1
  171.6 2.4 copy-start.1
  186.3 2.4 copy-start.1
  200.9 2.4 copy-start.1
Sparse Core Ops, SparseCore 0:
  39.4 46.3 all-gather.7
  87.6 41.1 all-gather.5
where the time goes:
time: 247 us; the launch traced here: 245 us
  matrix products  63.3 us (26%)
  waiting for transfers between devices  58.4 us (24%)
  blocking collectives  49.1 us (20%)
  local copies, waits for them, and re-layouts  32.5 us (13%)
  other arithmetic  25.9 us (10%)
  between operations  14.3 us (6%)
    all_gather x2, waiting for transfers between devices, prefix(): gathered = jax.tree.map(lambda a: lax.all_gather(a, axis), part)  58.3 us
    all_to_all x1, blocking collectives, per_device(): lax.all_to_all(rows, 'head', split_axis=0, concat_axis=1, tiled=True)  27.9 us
    all_gather x1, blocking collectives, prefix(): gathered = jax.tree.map(lambda a: lax.all_gather(a, axis), part)  21.2 us
    add x15, other arithmetic, combine(): later[0][:, None, None] * earlier[1] + later[1]  15.9 us
    dot_general x4, matrix products, block_grads(): jnp.einsum('hts,shn->thn', weighted, writes, precision=highest)  8.7 us
    dot_general x4, matrix products, finish(): jnp.einsum('thp,shp->hts', ups, ins, preferred_element_type=jnp.float32)  7.02 us
    dot_general x4, matrix products, block_grads(): through = jnp.einsum('htu,uhp->thp', coupled, upstream, precision=highest)  6.84 us
    dot_general x4, matrix products, block_grads(): jnp.einsum('thp,hpn->thn', inputs, adjoint_out, precision=highest)  6.69 us
  transfers between devices with their start and end apart: 2, of which 2 were waited for; matrix products, arithmetic and copies ran while one was open for 4% of the time, Pallas kernels for 0%

commit v1 on v0

v1 whole, which is shorter than its diff:
```python
import jax
import jax.numpy as jnp
from jax import lax
from jax.experimental import pallas as pl
from jax.experimental.pallas import tpu as pltpu
from jax.sharding import PartitionSpec as P

HEADS = 128
HEAD_SIZE = 64
STATE = 128
GROUPS = 8
TOKENS_DEV = 1024
HEADS_DEV = 8
FEATS = HEADS_DEV * HEAD_SIZE
CHUNK = 256
CHUNKS = TOKENS_DEV // CHUNK
CHIPS = 8
FAR = CHIPS // 2

f32 = jnp.float32
bf16 = jnp.bfloat16
VMEM_LIMIT = 40 * 1024 * 1024


def nn(a, b):
    return lax.dot_general(a, b, (((1,), (0,)), ((), ())), preferred_element_type=f32)


def nt(a, b):
    return lax.dot_general(a, b, (((1,), (1,)), ((), ())), preferred_element_type=f32)


def tn(a, b):
    return lax.dot_general(a, b, (((0,), (0,)), ((), ())), preferred_element_type=f32)


def halves(x):
    high = x.astype(bf16)
    return high, (x - high.astype(f32)).astype(bf16)


def head_columns():
    row = lax.broadcasted_iota(jnp.int32, (3 * HEADS_DEV, FEATS), 0) % HEADS_DEV
    col = lax.broadcasted_iota(jnp.int32, (3 * HEADS_DEV, FEATS), 1) // HEAD_SIZE
    return jnp.where(row == col, 1.0, 0.0).astype(bf16)


def spread(per_head, columns):
    high = per_head.astype(bf16).astype(f32)
    rest = per_head - high
    mid = rest.astype(bf16).astype(f32)
    low = rest - mid
    return tn(jnp.concatenate([high, mid, low], axis=0).astype(bf16), columns)


def head_vector(ref):
    row = lax.broadcasted_iota(jnp.int32, (HEADS_DEV, STATE), 0)
    out = jnp.zeros((HEADS_DEV, STATE), f32)
    for h in range(HEADS_DEV):
        out = jnp.where(row == h, ref[h], out)
    return out


def cumulate(x):
    lane = lax.broadcasted_iota(jnp.int32, x.shape, 1)
    hop = 1
    while hop < x.shape[1]:
        x = x + jnp.where(lane >= hop, pltpu.roll(x, hop, 1), 0.0)
        hop *= 2
    return x


def rows_of(i):
    return pl.ds(i * CHUNK, CHUNK)


def sums_kernel(
    u_hbm, dy_hbm, w_hbm, r_hbm, step_ref, rate_ref,
    out_ref, xdh_ref, xdl_ref, xuh_ref, xul_ref, dy_ref, w_ref, r_ref, bt_ref,
    u_ref, sems,
):
    column = pl.multiple_of(lax.axis_index("head") // 2 * STATE, STATE)
    copies = []
    for i in range(CHUNKS):
        rows = rows_of(i)
        group = [
            pltpu.make_async_copy(u_hbm.at[rows, :], u_ref.at[rows, :], sems.at[i, 0]),
            pltpu.make_async_copy(dy_hbm.at[rows, :], dy_ref.at[rows, :], sems.at[i, 1]),
            pltpu.make_async_copy(w_hbm.at[rows, pl.ds(column, STATE)], w_ref.at[rows, :], sems.at[i, 2]),
            pltpu.make_async_copy(r_hbm.at[rows, pl.ds(column, STATE)], r_ref.at[rows, :], sems.at[i, 3]),
        ]
        for copy in group:
            copy.start()
        copies.append(group)
    columns = head_columns()
    steps = step_ref[...]
    rate = head_vector(rate_ref)[:, :1]
    cum = cumulate(-steps * rate)
    last = cum[:, TOKENS_DEV - 1 :]
    middle = 0.5 * last
    ahead = jnp.exp(cum - middle)
    behind = jnp.exp(middle - cum) * steps
    bt_ref[...] = behind
    wide = lambda x: spread(jnp.broadcast_to(x, (HEADS_DEV, STATE)), columns)
    half = wide(jnp.exp(middle))
    acc_w = jnp.zeros((STATE, FEATS), f32)
    acc_r = jnp.zeros((STATE, FEATS), f32)
    for i in range(CHUNKS):
        rows = rows_of(i)
        for copy in copies[i]:
            copy.wait()
        high, low = halves(spread(behind[:, i * CHUNK : (i + 1) * CHUNK], columns) * u_ref[rows, :].astype(f32))
        xuh_ref[rows, :] = high
        xul_ref[rows, :] = low
        writes = w_ref[rows, :]
        acc_w = acc_w + tn(writes, high) + tn(writes, low)
        high, low = halves(spread(ahead[:, i * CHUNK : (i + 1) * CHUNK], columns) * dy_ref[rows, :].astype(f32))
        xdh_ref[rows, :] = high
        xdl_ref[rows, :] = low
        reads = r_ref[rows, :]
        acc_r = acc_r + tn(reads, high) + tn(reads, low)
    out_ref[pl.ds(0, STATE), :] = half * acc_w
    out_ref[pl.ds(STATE, STATE), :] = half * acc_r
    out_ref[pl.ds(2 * STATE, 8), :] = wide(last)[:8, :]


def message_kernel(own_ref, other_ref, a_ref, b_ref, c_ref, far_ref, w_ref, r_ref):
    place = lax.axis_index("ctx")
    chip, core = place // 2, place % 2
    own_log = own_ref[pl.ds(2 * STATE, 1), :]
    other_log = other_ref[pl.ds(2 * STATE, 1), :]
    own_decay = jnp.exp(own_log)
    other_decay = jnp.exp(other_log)
    first = core == 0
    one = jnp.ones_like(own_decay)
    w_ref[...] = (
        jnp.where(first, other_decay, one) * own_ref[pl.ds(0, STATE), :]
        + jnp.where(first, one, own_decay) * other_ref[pl.ds(0, STATE), :]
    )
    r_ref[...] = (
        jnp.where(first, one, other_decay) * own_ref[pl.ds(STATE, STATE), :]
        + jnp.where(first, own_decay, one) * other_ref[pl.ds(STATE, STATE), :]
    )
    logs = jnp.broadcast_to(own_log + other_log, (8, FEATS))
    for hop, ref in ((1, a_ref), (2, b_ref), (3, c_ref)):
        to_later = jnp.where(first, chip + hop < CHIPS, chip - hop < 0)

        @pl.when(to_later)
        def _():
            ref[pl.ds(0, STATE), :] = w_ref[...]

        @pl.when(jnp.logical_not(to_later))
        def _():
            ref[pl.ds(0, STATE), :] = r_ref[...]

        ref[pl.ds(STATE, 8), :] = logs
    half = FEATS // 2
    later = chip < FAR
    for part in range(2):
        cols = pl.ds(part * half, half)

        @pl.when(jnp.logical_and(later, core == part))
        def _():
            far_ref[pl.ds(0, STATE), :] = w_ref[:, cols]

        @pl.when(jnp.logical_and(jnp.logical_not(later), core == part))
        def _():
            far_ref[pl.ds(0, STATE), :] = r_ref[:, cols]

        @pl.when(core == part)
        def _():
            far_ref[pl.ds(STATE, 8), :] = logs[:, part * half : (part + 1) * half]


def local_kernel(
    xdh_ref, xdl_ref, xuh_ref, xul_ref, dy_ref, w_ref, r_ref, bt_ref, skip_ref, init_ref,
    gi_ref, back_ref, pw_ref, pr_ref, init_t_ref,
):
    columns = head_columns()
    skip = spread(head_vector(skip_ref), columns)[:1, :]
    init_t_ref[...] = init_ref[...].reshape(FEATS, STATE).T
    row = lax.broadcasted_iota(jnp.int32, (CHUNK, CHUNK), 0)
    col = lax.broadcasted_iota(jnp.int32, (CHUNK, CHUNK), 1)
    keep = col >= row
    for j in range(CHUNKS):
        to = rows_of(j)
        writes = w_ref[to, :]
        uh, ul = xuh_ref[to, :], xul_ref[to, :]
        acc_gi = jnp.zeros((CHUNK, FEATS), f32)
        acc_pw = jnp.zeros((CHUNK, STATE), f32)
        for i in range(j, CHUNKS):
            at = rows_of(i)
            dh, dl = xdh_ref[at, :], xdl_ref[at, :]
            reads = r_ref[at, :]
            pairs = nt(uh, dh) + nt(uh, dl) + nt(ul, dh)
            dots = nt(writes, reads)
            if i == j:
                pairs = jnp.where(keep, pairs, 0.0)
                dots = jnp.where(keep, dots, 0.0)
            ph, plow = halves(pairs)
            gh, gl = halves(dots)
            acc_pw = acc_pw + nn(ph, reads) + nn(plow, reads)
            part = tn(ph, writes) + tn(plow, writes)
            pr_ref[at, :] = part if j == 0 else pr_ref[at, :] + part
            acc_gi = acc_gi + nn(gh, dh) + nn(gh, dl) + nn(gl, dh)
        back = spread(bt_ref[:, j * CHUNK : (j + 1) * CHUNK], columns)
        back_ref[to, :] = back
        gi_ref[to, :] = back * acc_gi + skip * dy_ref[to, :].astype(f32)
        pw_ref[to, :] = acc_pw


def finish_kernel(
    own_ref, other_ref, a_ref, b_ref, c_ref, far_ref, oa_ref, ob_ref, oc_ref, ofar_ref,
    xdh_ref, xdl_ref, xuh_ref, xul_ref, w_ref, gi_ref, back_ref, pw_ref, pr_ref, init_t_ref,
    rows_ref, s_ref, t_ref,
):
    place = lax.axis_index("ctx")
    chip, core = place // 2, place % 2
    first = core == 0

    def pick(rows, hop):
        mine = (a_ref, b_ref, c_ref)[hop - 1][rows, :]
        theirs = (oa_ref, ob_ref, oc_ref)[hop - 1][rows, :]
        return jnp.where(first, mine, theirs), jnp.where(first, theirs, mine)

    def pick_far(rows):
        mine, theirs = far_ref[rows, :], ofar_ref[rows, :]
        return jnp.concatenate(
            [jnp.where(first, mine, theirs), jnp.where(first, theirs, mine)], axis=1
        )

    def distant(rows):
        below, above = {}, {}
        for hop in range(1, FAR):
            low, high = pick(rows, hop)
            below[hop], above[CHIPS - hop] = low, low
            above[hop], below[CHIPS - hop] = high, high
        middle = pick_far(rows)
        below[FAR], above[FAR] = middle, middle
        return below, above

    below_log, above_log = distant(pl.ds(STATE, 1))
    weights_s, weights_a = {}, {}
    total = jnp.zeros((1, FEATS), f32)
    for hop in range(1, CHIPS):
        valid = chip - hop >= 0
        weights_s[hop] = jnp.where(valid, jnp.exp(total), 0.0)
        total = total + jnp.where(valid, below_log[hop], 0.0)
    weight_init = jnp.exp(total)
    total = jnp.zeros((1, FEATS), f32)
    for hop in range(1, CHIPS):
        valid = chip + hop < CHIPS
        weights_a[hop] = jnp.where(valid, jnp.exp(total), 0.0)
        total = total + jnp.where(valid, above_log[hop], 0.0)

    own_log = own_ref[pl.ds(2 * STATE, 1), :]
    other_decay = jnp.exp(other_ref[pl.ds(2 * STATE, 1), :])
    half = jnp.exp(0.5 * own_log)
    for at in range(0, STATE, 32):
        rows = pl.ds(at, 32)
        below, above = distant(rows)
        state = weight_init * init_t_ref[rows, :]
        adjoint = jnp.zeros((32, FEATS), f32)
        for hop in range(1, CHIPS):
            state = state + weights_s[hop] * below[hop]
            adjoint = adjoint + weights_a[hop] * above[hop]
        state = jnp.where(first, state, other_ref[rows, :] + other_decay * state)
        adjoint = jnp.where(
            first, other_ref[pl.ds(STATE + at, 32), :] + other_decay * adjoint, adjoint
        )
        high, low = halves(half * state)
        s_ref[rows, :] = high
        s_ref[pl.ds(STATE + at, 32), :] = low
        high, low = halves(half * adjoint)
        t_ref[rows, :] = high
        t_ref[pl.ds(STATE + at, 32), :] = low

    for i in range(CHUNKS):
        rows = rows_of(i)
        reads = nt(xdh_ref[rows, :], s_ref[...])
        reads = reads[:, :STATE] + reads[:, STATE:] + nt(xdl_ref[rows, :], s_ref[pl.ds(0, STATE), :])
        writes = nt(xuh_ref[rows, :], t_ref[...])
        writes = writes[:, :STATE] + writes[:, STATE:] + nt(xul_ref[rows, :], t_ref[pl.ds(0, STATE), :])
        vectors = w_ref[rows, :]
        through = nn(jnp.concatenate([vectors, vectors], axis=1), t_ref[...])
        rows_ref[rows, pl.ds(0, FEATS)] = (gi_ref[rows, :] + back_ref[rows, :] * through).astype(bf16)
        rows_ref[rows, pl.ds(FEATS, STATE)] = (pw_ref[rows, :] + writes).astype(bf16)
        rows_ref[rows, pl.ds(FEATS + STATE, STATE)] = (pr_ref[rows, :] + reads).astype(bf16)


def arrange_kernel(in_ref, gi_ref, gw_ref, gr_ref):
    share = gi_ref.shape[0]
    peers = in_ref.shape[0] // share
    for j in range(peers):
        gi_ref[:, pl.ds(j * FEATS, FEATS)] = in_ref[pl.ds(j * share, share), pl.ds(0, FEATS)]
    for g in range(GROUPS):
        one, two = pl.ds(2 * g * share, share), pl.ds((2 * g + 1) * share, share)
        for ref, at in ((gw_ref, FEATS), (gr_ref, FEATS + STATE)):
            cols = pl.ds(at, STATE)
            ref[:, pl.ds(g * STATE, STATE)] = (
                in_ref[one, cols].astype(f32) + in_ref[two, cols].astype(f32)
            ).astype(bf16)


def call(body, outs, ins, scratch=(), flops=0):
    return pl.pallas_call(
        body,
        out_shape=outs,
        in_specs=ins,
        scratch_shapes=scratch,
        compiler_params=pltpu.CompilerParams(vmem_limit_bytes=VMEM_LIMIT),
        cost_estimate=pl.CostEstimate(flops=flops, bytes_accessed=1 << 20, transcendentals=0),
    )


IN_HBM = pl.BlockSpec(memory_space=pl.ANY)
IN_VMEM = pl.BlockSpec(memory_space=pltpu.VMEM)
IN_SMEM = pl.BlockSpec(memory_space=pltpu.SMEM)


def per_device(inputs, upstream, step_size, decay_rate, write_proj, read_proj, init_state, skip_gain):
    length = TOKENS_DEV
    wide = pltpu.VMEM((length, FEATS), bf16)
    wide32 = pltpu.VMEM((length, FEATS), f32)
    thin = pltpu.VMEM((length, STATE), bf16)
    thin32 = pltpu.VMEM((length, STATE), f32)
    own, xdh, xdl, xuh, xul, dy, w, r, bt = call(
        sums_kernel,
        (
            pltpu.VMEM((2 * STATE + 8, FEATS), f32),
            wide, wide, wide, wide, wide, thin, thin,
            pltpu.VMEM((HEADS_DEV, length), f32),
        ),
        [IN_HBM, IN_HBM, IN_HBM, IN_HBM, IN_VMEM, IN_SMEM],
        [pltpu.VMEM((length, FEATS), bf16), pltpu.SemaphoreType.DMA((CHUNKS, 4))],
        flops=1 << 30,
    )(inputs, upstream, write_proj, read_proj, step_size.T, decay_rate)

    swap = [(i, i ^ 1) for i in range(2 * CHIPS)]

    def fan(hop):
        up = [(2 * z, 2 * ((z + hop) % CHIPS)) for z in range(CHIPS)]
        down = [(2 * z + 1, 2 * ((z - hop) % CHIPS) + 1) for z in range(CHIPS)]
        return up + down

    other = lax.ppermute(own, "ctx", swap)
    message = jax.ShapeDtypeStruct((STATE + 8, FEATS), f32)
    messages = call(
        message_kernel,
        (message, message, message, jax.ShapeDtypeStruct((STATE + 8, FEATS // 2), f32)),
        [IN_VMEM, IN_VMEM],
        [pltpu.VMEM((STATE, FEATS), f32), pltpu.VMEM((STATE, FEATS), f32)],
        flops=1 << 20,
    )(own, other)
    mine = [lax.ppermute(m, "ctx", fan(hop)) for m, hop in zip(messages, (1, 2, 3, FAR))]
    theirs = [lax.ppermute(m, "ctx", swap) for m in mine]

    gi, back, pw, pr, init_t = call(
        local_kernel,
        (wide32, wide32, thin32, thin32, pltpu.VMEM((STATE, FEATS), f32)),
        [IN_VMEM] * 8 + [IN_SMEM, IN_VMEM],
        flops=5 << 30,
    )(xdh, xdl, xuh, xul, dy, w, r, bt, skip_gain, init_state)

    rows = call(
        finish_kernel,
        jax.ShapeDtypeStruct((length, FEATS + 2 * STATE), bf16),
        [IN_VMEM] * 20,
        [pltpu.VMEM((2 * STATE, FEATS), bf16), pltpu.VMEM((2 * STATE, FEATS), bf16)],
        flops=1 << 30,
    )(own, other, *mine, *theirs, xdh, xdl, xuh, xul, w, gi, back, pw, pr, init_t)

    moved = lax.all_to_all(rows, "head", split_axis=0, concat_axis=0, tiled=True)
    share = length // lax.axis_size("head")
    return call(
        arrange_kernel,
        (
            jax.ShapeDtypeStruct((share, HEADS * HEAD_SIZE), bf16),
            jax.ShapeDtypeStruct((share, GROUPS * STATE), bf16),
            jax.ShapeDtypeStruct((share, GROUPS * STATE), bf16),
        ),
        [IN_VMEM],
    )(moved)


def solution(mesh):
    placed = (
        P("ctx", "head"),
        P("ctx", "head"),
        P("ctx", "head"),
        P("head"),
        P("ctx", None),
        P("ctx", None),
        P("head", None, None),
        P("head"),
    )
    return jax.shard_map(
        per_device,
        mesh=mesh,
        in_specs=placed,
        out_specs=(P(("ctx", "head"), None), P(("ctx", "head"), None), P(("ctx", "head"), None)),
        check_vma=False,
    )
```

time: 247 us -> 90.2 us (0.37)
  the two profiles are of different devices: /device:TPU:1 before, /device:TPU:64 now
where the time goes in v1:
time: 90.2 us; the launch traced here: 89.9 us
  blocking collectives  30 us (33%)
  waiting for transfers between devices  22.8 us (25%)
  Pallas kernels  17.1 us (19%)
  starting transfers between devices  12.2 us (14%)
  local copies, waits for them, and re-layouts  7.04 us (8%)
    all_to_all x1, blocking collectives, per_device(): lax.all_to_all(rows, 'head', split_axis=0, concat_axis=0, tiled=True)  30 us
    ppermute x4, waiting for transfers between devices, per_device(): lax.ppermute(m, 'ctx', fan(hop))  20.8 us
    ppermute x4, starting transfers between devices, per_device(): lax.ppermute(m, 'ctx', fan(hop))  11.1 us
    pallas_call x1, Pallas kernels, per_device(): call(local_kernel, (wide32, wide32, thin32, thin32, pltpu.VMEM((STATE, FE...  9.11 us
    unnamed x16, local copies, waits for them, and re-layouts  7.04 us
    pallas_call x1, Pallas kernels, per_device(): call(sums_kernel, (pltpu.VMEM((2 * STATE + 8, FEATS), f32), wide, wide, w...  4.61 us
    pallas_call x1, Pallas kernels, per_device(): call(finish_kernel, jax.ShapeDtypeStruct((length, FEATS + 2 * STATE), bf1...  2.1 us
    ppermute x1, waiting for transfers between devices, per_device(): other = lax.ppermute(own, 'ctx', swap)  1.92 us
  transfers between devices with their start and end apart: 9, of which 2 were waited for; matrix products, arithmetic and copies ran while one was open for 0% of the time, Pallas kernels for 10%

profile of v1, /device:TPU:64, one launch (start us, length us, event | category | flops | bytes accessed | tf_op | source)
XLA Modules:
  0.0 89.9 jit_solution(18127414955272663272)
XLA Ops:
  0.6 1.6 %copy-done = bf16[1024,1024]{1,0:T(8,128)(2,1)S(1)} copy-done((bf16[1024,1024]{1,0:T(8,128)(2,1)S(1)}, bf16[1024,1024]{1,0:T(8,128)(2,1)}, u32[]{:S(2)}) %copy-start) | copy-done | bytes 2097176
  2.2 1.6 %copy-done.1 = bf16[1024,1024]{1,0:T(8,128)(2,1)S(1)} copy-done((bf16[1024,1024]{1,0:T(8,128)(2,1)S(1)}, bf16[1024,1024]{1,0:T(8,128)(2,1)}, u32[]{:S(2)}) %copy-start.1) | copy-done | bytes 2097176
  3.8 1.2 %copy-done.2 = bf16[1024,512]{1,0:T(8,128)(2,1)S(1)} copy-done((bf16[1024,512]{1,0:T(8,128)(2,1)S(1)}, bf16[1024,512]{1,0:T(8,128)(2,1)}, u32[]{:S(2)}) %copy-start.2) | copy-done | bytes 1048600
  5.0 1.2 %copy-done.3 = bf16[1024,512]{1,0:T(8,128)(2,1)S(1)} copy-done((bf16[1024,512]{1,0:T(8,128)(2,1)S(1)}, bf16[1024,512]{1,0:T(8,128)(2,1)}, u32[]{:S(2)}) %copy-start.3) | copy-done | bytes 1048600
  6.3 0.8 copy-done.4
  7.0 0.7 copy-done.5
  7.7 4.6 %shard_map.103 = (f32[264,512]{1,0:T(8,128)S(1)}, bf16[1024,512]{1,0:T(8,128)(2,1)S(1)}, bf16[1024,512]{1,0:T(8,128)(2,1)S(1)}, bf16[1024,512]{1,0:T(8,128)(2,1)...) custom-call(bf16[1024,512]{1,0:T(8,128)(2,1)S(1)} %copy-done.2, ...), custom_call_target="tpu_custom_call" | custom-call | flops 1073741824 | bytes 1048576 | tf_op jit(solution)/shard_map/pallas_call | solution.py:327
  12.3 0.1 collective-permute-start
  12.4 1.9 %collective-permute-done.other_ref = f32[264,512]{1,0:T(8,128)S(1)} collective-permute-done((f32[264,512]{1,0:T(8,128)S(1)}, f32[264,512]{1,0:T(8,128)S(1)}, u32[]{:S(2)}, u32[]{:S(2)}) %collective-permute-start) | collective-permute-done | bytes 540704 | tf_op jit(solution)/shard_map/ppermute | solution.py:346
  14.3 0.2 shard_map.104
  14.5 2.0 %collective-permute-start.1 = (f32[136,512]{1,0:T(8,128)S(1)}, f32[136,512]{1,0:T(8,128)S(1)}, u32[]{:S(2)}, u32[]{:S(2)}) collective-permute-start(f32[136,512]{1,0:T(8,128)S(1)} %get-tuple-element.22), channel_id=1, source_target_pairs={{0,32},{32,64},{64,96},{96,128},{128,160},{160,192},{192,224},{224... | collective-permute-start | bytes 835592 | tf_op jit(solution)/shard_map/ppermute | solution.py:355
  16.5 3.6 %collective-permute-start.2 = (f32[136,512]{1,0:T(8,128)S(1)}, f32[136,512]{1,0:T(8,128)S(1)}, u32[]{:S(2)}, u32[]{:S(2)}) collective-permute-start(f32[136,512]{1,0:T(8,128)S(1)} %get-tuple-element.23), channel_id=1, source_target_pairs={{0,64},{32,96},{64,128},{96,160},{128,192},{160,224},{192,0},{224,... | collective-permute-start | bytes 835592 | tf_op jit(solution)/shard_map/ppermute | solution.py:355
  20.1 1.0 %collective-permute-start.3 = (f32[136,512]{1,0:T(8,128)S(1)}, f32[136,512]{1,0:T(8,128)S(1)}, u32[]{:S(2)}, u32[]{:S(2)}) collective-permute-start(f32[136,512]{1,0:T(8,128)S(1)} %get-tuple-element.24), channel_id=1, source_target_pairs={{0,96},{32,128},{64,160},{96,192},{128,224},{160,0},{192,32},{224,... | collective-permute-start | bytes 835592 | tf_op jit(solution)/shard_map/ppermute | solution.py:355
  21.1 4.5 %collective-permute-start.4 = (f32[136,256]{1,0:T(8,128)S(1)}, f32[136,256]{1,0:T(8,128)S(1)}, u32[]{:S(2)}, u32[]{:S(2)}) collective-permute-start(f32[136,256]{1,0:T(8,128)S(1)} %get-tuple-element.25), channel_id=1, source_target_pairs={{0,128},{32,160},{64,192},{96,224},{128,0},{160,32},{192,64},{224,... | collective-permute-start | bytes 417800 | tf_op jit(solution)/shard_map/ppermute | solution.py:355
  25.6 20.8 %collective-permute-done.4.far_ref = f32[136,256]{1,0:T(8,128)S(1)} collective-permute-done((f32[136,256]{1,0:T(8,128)S(1)}, f32[136,256]{1,0:T(8,128)S(1)}, u32[]{:S(2)}, u32[]{:S(2)}) %collective-permute-start.4) | collective-permute-done | bytes 139296 | tf_op jit(solution)/shard_map/ppermute | solution.py:355
  46.4 0.0 collective-permute-start.8
  46.4 0.5 collective-permute-start.5
  46.9 0.1 collective-permute-start.6
  47.0 0.0 collective-permute-done.3.c_ref
  47.0 0.4 collective-permute-start.7
  47.4 9.1 %shard_map.105 = (f32[1024,512]{1,0:T(8,128)S(1)}, f32[1024,512]{1,0:T(8,128)S(1)}, f32[1024,128]{1,0:T(8,128)S(1)}, f32[1024,128]{1,0:T(8,128)S(1)}, f32[128,512]{1,0:T(8,128)S(1)}) custom-call(bf16[1024,512]{1,0:T(8,128)(2,1)S(1)} %get-tuple-element.26.xdh_ref, bf16[1024,512]{1,0:T(8,128)(2,1)S(1)} %get-tuple-element.27.xdl_ref, ...), custom_call_target="tpu_custom_call" | custom-call | flops 5368709120 | bytes 1048576 | tf_op jit(solution)/shard_map/pallas_call | solution.py:358
  56.6 2.1 %shard_map.106 = bf16[1024,768]{1,0:T(8,128)(2,1)S(1)} custom-call(f32[264,512]{1,0:T(8,128)S(1)} %get-tuple-element.21.own_ref, f32[264,512]{1,0:T(8,128)S(1)} %collective-permute-done.other_ref, f32[136,512]{1,0:T(8,128)S(1)} %collective-permute-done.1.a_ref, f32[136,512]{1,0:T(8,128)S(1)} %collective-permute-done.2.b_ref, ...), custom_call_target="tpu_custom_call" | custom-call | flops 1073741824 | bytes 1048576 | tf_op jit(solution)/shard_map/pallas_call | solution.py:365
  58.7 30.0 %all_to_all.11 = bf16[16,64,768]{2,1,0:T(8,128)(2,1)S(1)} all-to-all(bf16[16,64,768]{2,1,0:T(8,128)(2,1)S(1)} %bitcast.4), channel_id=1, replica_groups=mesh['ctx'=16,'head'=16] {'head'}, dimensions={0} | all-to-all | bytes 3145728 | tf_op jit(solution)/shard_map/all_to_all | solution.py:373
  88.7 1.1 %shard_map.107 = (bf16[64,8192]{1,0:T(8,128)(2,1)}, bf16[64,1024]{1,0:T(8,128)(2,1)}, bf16[64,1024]{1,0:T(8,128)(2,1)}) custom-call(bf16[1024,768]{1,0:T(8,128)(2,1)S(1)} %bitcast.3), custom_call_target="tpu_custom_call" | custom-call | bytes 1048576 | tf_op jit(solution)/shard_map/pallas_call | solution.py:375
  (16 shorter events, 0.0 us)
Async XLA Ops:
  0.6 1.6 %copy-start = (bf16[1024,1024]{1,0:T(8,128)(2,1)S(1)}, bf16[1024,1024]{1,0:T(8,128)(2,1)}, u32[]{:S(2)}) copy-start(bf16[1024,1024]{1,0:T(8,128)(2,1)} %w_hbm.1) | copy-start | bytes 6291460
  2.2 1.6 %copy-start.1 = (bf16[1024,1024]{1,0:T(8,128)(2,1)S(1)}, bf16[1024,1024]{1,0:T(8,128)(2,1)}, u32[]{:S(2)}) copy-start(bf16[1024,1024]{1,0:T(8,128)(2,1)} %r_hbm.1) | copy-start | bytes 6291460
  3.8 1.2 %copy-start.2 = (bf16[1024,512]{1,0:T(8,128)(2,1)S(1)}, bf16[1024,512]{1,0:T(8,128)(2,1)}, u32[]{:S(2)}) copy-start(bf16[1024,512]{1,0:T(8,128)(2,1)} %u_hbm.1) | copy-start | bytes 3145732
  5.0 1.2 %copy-start.3 = (bf16[1024,512]{1,0:T(8,128)(2,1)S(1)}, bf16[1024,512]{1,0:T(8,128)(2,1)}, u32[]{:S(2)}) copy-start(bf16[1024,512]{1,0:T(8,128)(2,1)} %dy_hbm.1) | copy-start | bytes 3145732
  6.3 0.8 copy-start.4
  7.0 0.7 copy-start.5
  7.7 39.8 %copy-start.6 = (f32[8,64,128]{2,1,0:T(8,128)S(1)}, f32[8,64,128]{2,1,0:T(8,128)}, u32[]{:S(2)}) copy-start(f32[8,64,128]{2,1,0:T(8,128)} %init_ref.1) | copy-start | bytes 786436
  7.7 39.8 %copy-start.7 = (f32[8]{0:T(128)S(1)}, f32[8]{0:T(128)}, u32[]{:S(2)}) copy-start(f32[8]{0:T(128)} %skip_ref.1) | copy-start | bytes 100
  12.3 2.0 %collective-permute-start = (f32[264,512]{1,0:T(8,128)S(1)}, f32[264,512]{1,0:T(8,128)S(1)}, u32[]{:S(2)}, u32[]{:S(2)}) collective-permute-start(f32[264,512]{1,0:T(8,128)S(1)} %get-tuple-element.21.own_ref), channel_id=1, source_target_pairs={{0,16},{16,0},{32,48},{48,32},{64,80},{80,64},{96,112},{112,96},{1... | collective-permute-start | bytes 1622024 | tf_op jit(solution)/shard_map/ppermute | solution.py:346
  14.5 31.9 %collective-permute-start.1 = (f32[136,512]{1,0:T(8,128)S(1)}, f32[136,512]{1,0:T(8,128)S(1)}, u32[]{:S(2)}, u32[]{:S(2)}) collective-permute-start(f32[136,512]{1,0:T(8,128)S(1)} %get-tuple-element.22), channel_id=1, source_target_pairs={{0,32},{32,64},{64,96},{96,128},{128,160},{160,192},{192,224},{224... | collective-permute-start | bytes 835592 | tf_op jit(solution)/shard_map/ppermute | solution.py:355
  16.5 30.4 %collective-permute-start.2 = (f32[136,512]{1,0:T(8,128)S(1)}, f32[136,512]{1,0:T(8,128)S(1)}, u32[]{:S(2)}, u32[]{:S(2)}) collective-permute-start(f32[136,512]{1,0:T(8,128)S(1)} %get-tuple-element.23), channel_id=1, source_target_pairs={{0,64},{32,96},{64,128},{96,160},{128,192},{160,224},{192,0},{224,... | collective-permute-start | bytes 835592 | tf_op jit(solution)/shard_map/ppermute | solution.py:355
  20.1 26.9 %collective-permute-start.3 = (f32[136,512]{1,0:T(8,128)S(1)}, f32[136,512]{1,0:T(8,128)S(1)}, u32[]{:S(2)}, u32[]{:S(2)}) collective-permute-start(f32[136,512]{1,0:T(8,128)S(1)} %get-tuple-element.24), channel_id=1, source_target_pairs={{0,96},{32,128},{64,160},{96,192},{128,224},{160,0},{192,32},{224,... | collective-permute-start | bytes 835592 | tf_op jit(solution)/shard_map/ppermute | solution.py:355
  21.1 25.3 %collective-permute-start.4 = (f32[136,256]{1,0:T(8,128)S(1)}, f32[136,256]{1,0:T(8,128)S(1)}, u32[]{:S(2)}, u32[]{:S(2)}) collective-permute-start(f32[136,256]{1,0:T(8,128)S(1)} %get-tuple-element.25), channel_id=1, source_target_pairs={{0,128},{32,160},{64,192},{96,224},{128,0},{160,32},{192,64},{224,... | collective-permute-start | bytes 417800 | tf_op jit(solution)/shard_map/ppermute | solution.py:355
  46.4 10.2 %collective-permute-start.8 = (f32[136,256]{1,0:T(8,128)S(1)}, f32[136,256]{1,0:T(8,128)S(1)}, u32[]{:S(2)}, u32[]{:S(2)}) collective-permute-start(f32[136,256]{1,0:T(8,128)S(1)} %collective-permute-done.4.far_ref), channel_id=1, source_target_pairs={{0,16},{16,0},{32,48},{48,32},{64,80},{80,64},{96,112},{112,96},{1... | collective-permute-start | bytes 417800 | tf_op jit(solution)/shard_map/ppermute | solution.py:356
  46.4 10.2 %collective-permute-start.5 = (f32[136,512]{1,0:T(8,128)S(1)}, f32[136,512]{1,0:T(8,128)S(1)}, u32[]{:S(2)}, u32[]{:S(2)}) collective-permute-start(f32[136,512]{1,0:T(8,128)S(1)} %collective-permute-done.1.a_ref), channel_id=1, source_target_pairs={{0,16},{16,0},{32,48},{48,32},{64,80},{80,64},{96,112},{112,96},{1... | collective-permute-start | bytes 835592 | tf_op jit(solution)/shard_map/ppermute | solution.py:356
  46.9 9.7 %collective-permute-start.6 = (f32[136,512]{1,0:T(8,128)S(1)}, f32[136,512]{1,0:T(8,128)S(1)}, u32[]{:S(2)}, u32[]{:S(2)}) collective-permute-start(f32[136,512]{1,0:T(8,128)S(1)} %collective-permute-done.2.b_ref), channel_id=1, source_target_pairs={{0,16},{16,0},{32,48},{48,32},{64,80},{80,64},{96,112},{112,96},{1... | collective-permute-start | bytes 835592 | tf_op jit(solution)/shard_map/ppermute | solution.py:356
  47.0 9.6 %collective-permute-start.7 = (f32[136,512]{1,0:T(8,128)S(1)}, f32[136,512]{1,0:T(8,128)S(1)}, u32[]{:S(2)}, u32[]{:S(2)}) collective-permute-start(f32[136,512]{1,0:T(8,128)S(1)} %collective-permute-done.3.c_ref), channel_id=1, source_target_pairs={{0,16},{16,0},{32,48},{48,32},{64,80},{80,64},{96,112},{112,96},{1... | collective-permute-start | bytes 835592 | tf_op jit(solution)/shard_map/ppermute | solution.py:356

commit v2 on v1

--- a/solution.py
+++ b/solution.py
@@ -1,3 +1,5 @@
+import functools
+
 import jax
 import jax.numpy as jnp
 from jax import lax
@@ -16,6 +18,9 @@
 CHUNKS = TOKENS_DEV // CHUNK
 CHIPS = 8
 FAR = CHIPS // 2
+ROWS = STATE + 16
+LEAST = 1e-30
+CUT = 2
 
 f32 = jnp.float32
 bf16 = jnp.bfloat16
@@ -75,11 +80,17 @@
 
 
 def sums_kernel(
-    u_hbm, dy_hbm, w_hbm, r_hbm, step_ref, rate_ref,
+    u_hbm, dy_hbm, w_hbm, r_hbm, step_hbm, rate_hbm,
     out_ref, xdh_ref, xdl_ref, xuh_ref, xul_ref, dy_ref, w_ref, r_ref, bt_ref,
-    u_ref, sems,
+    u_ref, step_ref, rate_ref, sems,
 ):
     column = pl.multiple_of(lax.axis_index("head") // 2 * STATE, STATE)
+    small = [
+        pltpu.make_async_copy(step_hbm, step_ref, sems.at[CHUNKS, 0]),
+        pltpu.make_async_copy(rate_hbm, rate_ref, sems.at[CHUNKS, 1]),
+    ]
+    for copy in small:
+        copy.start()
     copies = []
     for i in range(CHUNKS):
         rows = rows_of(i)
@@ -93,6 +104,8 @@
             copy.start()
         copies.append(group)
     columns = head_columns()
+    for copy in small:
+        copy.wait()
     steps = step_ref[...]
     rate = head_vector(rate_ref)[:, :1]
     cum = cumulate(-steps * rate)
@@ -124,6 +137,12 @@
     out_ref[pl.ds(2 * STATE, 8), :] = wide(last)[:8, :]
 
 
+def parts_of(x):
+    high = x.astype(bf16).astype(f32)
+    mid = (x - high).astype(bf16).astype(f32)
+    return [high, mid, x - high - mid]
+
+
 def message_kernel(own_ref, other_ref, a_ref, b_ref, c_ref, far_ref, w_ref, r_ref):
     place = lax.axis_index("ctx")
     chip, core = place // 2, place % 2
@@ -133,27 +152,29 @@
     other_decay = jnp.exp(other_log)
     first = core == 0
     one = jnp.ones_like(own_decay)
-    w_ref[...] = (
-        jnp.where(first, other_decay, one) * own_ref[pl.ds(0, STATE), :]
-        + jnp.where(first, one, own_decay) * other_ref[pl.ds(0, STATE), :]
-    )
-    r_ref[...] = (
-        jnp.where(first, one, other_decay) * own_ref[pl.ds(STATE, STATE), :]
-        + jnp.where(first, own_decay, one) * other_ref[pl.ds(STATE, STATE), :]
-    )
-    logs = jnp.broadcast_to(own_log + other_log, (8, FEATS))
+    logs = parts_of(own_log + other_log)
+    for ref, left, right, at in (
+        (w_ref, jnp.where(first, other_decay, one), jnp.where(first, one, own_decay), 0),
+        (r_ref, jnp.where(first, one, other_decay), jnp.where(first, own_decay, one), STATE),
+    ):
+        rows = pl.ds(at, STATE)
+        total = left * own_ref[rows, :] + right * other_ref[rows, :]
+        scale = jnp.maximum(jnp.max(jnp.abs(total), axis=0, keepdims=True), LEAST)
+        ref[pl.ds(0, STATE), :] = total * (1.0 / scale)
+        ref[pl.ds(STATE, 16), :] = jnp.concatenate(
+            logs + parts_of(jnp.log(scale)) + [jnp.zeros((10, FEATS), f32)], axis=0
+        )
     for hop, ref in ((1, a_ref), (2, b_ref), (3, c_ref)):
         to_later = jnp.where(first, chip + hop < CHIPS, chip - hop < 0)
 
         @pl.when(to_later)
         def _():
-            ref[pl.ds(0, STATE), :] = w_ref[...]
+            ref[...] = w_ref[...]
 
         @pl.when(jnp.logical_not(to_later))
         def _():
-            ref[pl.ds(0, STATE), :] = r_ref[...]
-
-        ref[pl.ds(STATE, 8), :] = logs
+            ref[...] = r_ref[...]
+
     half = FEATS // 2
     later = chip < FAR
     for part in range(2):
@@ -161,35 +182,33 @@
 
         @pl.when(jnp.logical_and(later, core == part))
         def _():
-            far_ref[pl.ds(0, STATE), :] = w_ref[:, cols]
+            far_ref[...] = w_ref[:, cols]
 
         @pl.when(jnp.logical_and(jnp.logical_not(later), core == part))
         def _():
-            far_ref[pl.ds(0, STATE), :] = r_ref[:, cols]
-
-        @pl.when(core == part)
-        def _():
-            far_ref[pl.ds(STATE, 8), :] = logs[:, part * half : (part + 1) * half]
-
-
-def local_kernel(
-    xdh_ref, xdl_ref, xuh_ref, xul_ref, dy_ref, w_ref, r_ref, bt_ref, skip_ref, init_ref,
-    gi_ref, back_ref, pw_ref, pr_ref, init_t_ref,
-):
+            far_ref[...] = r_ref[:, cols]
+
+
+def local_kernel(parts, *refs):
+    first = 0 in parts
+    xdh_ref, xdl_ref, xuh_ref, xul_ref, dy_ref, w_ref, r_ref, bt_ref, skip_ref = refs[:9]
+    gi_ref, back_ref, pw_ref, pr_ref = refs[10:14]
     columns = head_columns()
     skip = spread(head_vector(skip_ref), columns)[:1, :]
-    init_t_ref[...] = init_ref[...].reshape(FEATS, STATE).T
+    if first:
+        refs[14][...] = refs[9][...].reshape(FEATS, STATE).T
     row = lax.broadcasted_iota(jnp.int32, (CHUNK, CHUNK), 0)
     col = lax.broadcasted_iota(jnp.int32, (CHUNK, CHUNK), 1)
     keep = col >= row
-    for j in range(CHUNKS):
-        to = rows_of(j)
+    base = parts[0]
+    for j in parts:
+        to, out = rows_of(j), rows_of(j - base)
         writes = w_ref[to, :]
         uh, ul = xuh_ref[to, :], xul_ref[to, :]
         acc_gi = jnp.zeros((CHUNK, FEATS), f32)
         acc_pw = jnp.zeros((CHUNK, STATE), f32)
         for i in range(j, CHUNKS):
-            at = rows_of(i)
+            at, into = rows_of(i), rows_of(i - base)
             dh, dl = xdh_ref[at, :], xdl_ref[at, :]
             reads = r_ref[at, :]
             pairs = nt(uh, dh) + nt(uh, dl) + nt(ul, dh)
@@ -201,18 +220,18 @@
             gh, gl = halves(dots)
             acc_pw = acc_pw + nn(ph, reads) + nn(plow, reads)
             part = tn(ph, writes) + tn(plow, writes)
-            pr_ref[at, :] = part if j == 0 else pr_ref[at, :] + part
+            pr_ref[into, :] = part if j == base else pr_ref[into, :] + part
             acc_gi = acc_gi + nn(gh, dh) + nn(gh, dl) + nn(gl, dh)
         back = spread(bt_ref[:, j * CHUNK : (j + 1) * CHUNK], columns)
-        back_ref[to, :] = back
-        gi_ref[to, :] = back * acc_gi + skip * dy_ref[to, :].astype(f32)
-        pw_ref[to, :] = acc_pw
+        back_ref[out, :] = back
+        gi_ref[out, :] = back * acc_gi + skip * dy_ref[to, :].astype(f32)
+        pw_ref[out, :] = acc_pw
 
 
 def finish_kernel(
     own_ref, other_ref, a_ref, b_ref, c_ref, far_ref, oa_ref, ob_ref, oc_ref, ofar_ref,
-    xdh_ref, xdl_ref, xuh_ref, xul_ref, w_ref, gi_ref, back_ref, pw_ref, pr_ref, init_t_ref,
-    rows_ref, s_ref, t_ref,
+    xdh_ref, xdl_ref, xuh_ref, xul_ref, w_ref, gi1_ref, back1_ref, pw1_ref, pr1_ref, init_t_ref,
+    gi2_ref, back2_ref, pw2_ref, pr2_ref, rows_ref, s_ref, t_ref,
 ):
     place = lax.axis_index("ctx")
     chip, core = place // 2, place % 2
@@ -239,19 +258,25 @@
         below[FAR], above[FAR] = middle, middle
         return below, above
 
-    below_log, above_log = distant(pl.ds(STATE, 1))
+    below, above = distant(pl.ds(STATE, 8))
     weights_s, weights_a = {}, {}
+
+    def logs(rows):
+        return rows[0:1] + rows[1:2] + rows[2:3], rows[3:4] + rows[4:5] + rows[5:6]
+
     total = jnp.zeros((1, FEATS), f32)
     for hop in range(1, CHIPS):
         valid = chip - hop >= 0
-        weights_s[hop] = jnp.where(valid, jnp.exp(total), 0.0)
-        total = total + jnp.where(valid, below_log[hop], 0.0)
+        decay, scale = logs(below[hop])
+        weights_s[hop] = jnp.where(valid, jnp.exp(total + scale), 0.0)
+        total = total + jnp.where(valid, decay, 0.0)
     weight_init = jnp.exp(total)
     total = jnp.zeros((1, FEATS), f32)
     for hop in range(1, CHIPS):
         valid = chip + hop < CHIPS
-        weights_a[hop] = jnp.where(valid, jnp.exp(total), 0.0)
-        total = total + jnp.where(valid, above_log[hop], 0.0)
+        decay, scale = logs(above[hop])
+        weights_a[hop] = jnp.where(valid, jnp.exp(total + scale), 0.0)
+        total = total + jnp.where(valid, decay, 0.0)
 
     own_log = own_ref[pl.ds(2 * STATE, 1), :]
     other_decay = jnp.exp(other_ref[pl.ds(2 * STATE, 1), :])
@@ -283,9 +308,19 @@
         writes = writes[:, :STATE] + writes[:, STATE:] + nt(xul_ref[rows, :], t_ref[pl.ds(0, STATE), :])
         vectors = w_ref[rows, :]
         through = nn(jnp.concatenate([vectors, vectors], axis=1), t_ref[...])
-        rows_ref[rows, pl.ds(0, FEATS)] = (gi_ref[rows, :] + back_ref[rows, :] * through).astype(bf16)
-        rows_ref[rows, pl.ds(FEATS, STATE)] = (pw_ref[rows, :] + writes).astype(bf16)
-        rows_ref[rows, pl.ds(FEATS + STATE, STATE)] = (pr_ref[rows, :] + reads).astype(bf16)
+        early = i < CUT
+        gi_ref, back_ref, pw_ref = (gi1_ref, back1_ref, pw1_ref) if early else (gi2_ref, back2_ref, pw2_ref)
+        at = rows_of(i if early else i - CUT)
+        reads = reads + pr1_ref[rows, :]
+        if not early:
+            reads = reads + pr2_ref[at, :]
+        rows_ref[rows, pl.ds(0, FEATS)] = (gi_ref[at, :] + back_ref[at, :] * through).astype(bf16)
+        rows_ref[rows, pl.ds(FEATS, STATE)] = (pw_ref[at, :] + writes).astype(bf16)
+        rows_ref[rows, pl.ds(FEATS + STATE, STATE)] = reads.astype(bf16)
+
+
+def relay_kernel(*refs):
+    pass
 
 
 def arrange_kernel(in_ref, gi_ref, gw_ref, gr_ref):
@@ -313,7 +348,8 @@
     )
 
 
-IN_HBM = pl.BlockSpec(memory_space=pl.ANY)
+IN_HBM = pl.BlockSpec(memory_space=pltpu.HBM)
+IN_ANY = pl.BlockSpec(memory_space=pl.ANY)
 IN_VMEM = pl.BlockSpec(memory_space=pltpu.VMEM)
 IN_SMEM = pl.BlockSpec(memory_space=pltpu.SMEM)
 
@@ -331,10 +367,20 @@
             wide, wide, wide, wide, wide, thin, thin,
             pltpu.VMEM((HEADS_DEV, length), f32),
         ),
-        [IN_HBM, IN_HBM, IN_HBM, IN_HBM, IN_VMEM, IN_SMEM],
-        [pltpu.VMEM((length, FEATS), bf16), pltpu.SemaphoreType.DMA((CHUNKS, 4))],
+        [IN_HBM] * 6,
+        [
+            pltpu.VMEM((length, FEATS), bf16),
+            pltpu.VMEM((HEADS_DEV, length), f32),
+            pltpu.SMEM((HEADS_DEV,), f32),
+            pltpu.SemaphoreType.DMA((CHUNKS + 1, 4)),
+        ],
         flops=1 << 30,
-    )(inputs, upstream, write_proj, read_proj, step_size.T, decay_rate)
+    )(
+        *(
+            pltpu.with_memory_space_constraint(a, pltpu.HBM)
+            for a in (inputs, upstream, write_proj, read_proj, step_size.T, decay_rate)
+        )
+    )
 
     swap = [(i, i ^ 1) for i in range(2 * CHIPS)]
 
@@ -344,31 +390,49 @@
         return up + down
 
     other = lax.ppermute(own, "ctx", swap)
-    message = jax.ShapeDtypeStruct((STATE + 8, FEATS), f32)
+    message = jax.ShapeDtypeStruct((ROWS, FEATS), f32)
     messages = call(
         message_kernel,
-        (message, message, message, jax.ShapeDtypeStruct((STATE + 8, FEATS // 2), f32)),
+        (message, message, message, jax.ShapeDtypeStruct((ROWS, FEATS // 2), f32)),
         [IN_VMEM, IN_VMEM],
-        [pltpu.VMEM((STATE, FEATS), f32), pltpu.VMEM((STATE, FEATS), f32)],
+        [pltpu.VMEM((ROWS, FEATS), f32), pltpu.VMEM((ROWS, FEATS), f32)],
         flops=1 << 20,
     )(own, other)
-    mine = [lax.ppermute(m, "ctx", fan(hop)) for m, hop in zip(messages, (1, 2, 3, FAR))]
+    mine = [
+        lax.ppermute(m.astype(jnp.float16), "ctx", fan(hop)).astype(f32)
+        for m, hop in zip(messages, (1, 2, 3, FAR))
+    ]
+
+    def local(parts, flops):
+        out = lambda n, d: pltpu.VMEM((CHUNK * n, d), f32)
+        n = len(parts)
+        left = CHUNKS - parts[0]
+        outs = (out(n, FEATS), out(n, FEATS), out(n, STATE), out(left, STATE))
+        if 0 in parts:
+            outs = outs + (pltpu.VMEM((STATE, FEATS), f32),)
+        return call(
+            functools.partial(local_kernel, parts), outs, [IN_VMEM] * 8 + [IN_SMEM, IN_VMEM], flops=flops
+        )(xdh, xdl, xuh, xul, dy, w, r, bt, skip_gain, init_state)
+
+    early = local(tuple(range(CUT)), 4 << 30)
+    late = local(tuple(range(CUT, CHUNKS)), 2 << 30)
+    relayed = pl.pallas_call(
+        relay_kernel,
+        out_shape=tuple(jax.ShapeDtypeStruct(m.shape, m.dtype) for m in mine),
+        in_specs=[IN_ANY] * 5,
+        out_specs=(IN_ANY,) * 4,
+        input_output_aliases={i: i for i in range(4)},
+    )(*mine, early[2])
+    mine = list(relayed)
     theirs = [lax.ppermute(m, "ctx", swap) for m in mine]
-
-    gi, back, pw, pr, init_t = call(
-        local_kernel,
-        (wide32, wide32, thin32, thin32, pltpu.VMEM((STATE, FEATS), f32)),
-        [IN_VMEM] * 8 + [IN_SMEM, IN_VMEM],
-        flops=5 << 30,
-    )(xdh, xdl, xuh, xul, dy, w, r, bt, skip_gain, init_state)
 
     rows = call(
         finish_kernel,
         jax.ShapeDtypeStruct((length, FEATS + 2 * STATE), bf16),
-        [IN_VMEM] * 20,
+        [IN_VMEM] * 24,
         [pltpu.VMEM((2 * STATE, FEATS), bf16), pltpu.VMEM((2 * STATE, FEATS), bf16)],
         flops=1 << 30,
-    )(own, other, *mine, *theirs, xdh, xdl, xuh, xul, w, gi, back, pw, pr, init_t)
+    )(own, other, *mine, *theirs, xdh, xdl, xuh, xul, w, *early, *late)
 
     moved = lax.all_to_all(rows, "head", split_axis=0, concat_axis=0, tiled=True)
     share = length // lax.axis_size("head")

time: 90.2 us -> 77.7 us (0.86)
  the two profiles are of different devices: /device:TPU:64 before, /device:TPU:1 now
where the time goes in v2:
time: 77.7 us; the launch traced here: 77.4 us
  blocking collectives  29.1 us (37%)
  Pallas kernels  18.5 us (24%)
  starting transfers between devices  14.5 us (19%)
  local copies, waits for them, and re-layouts  9.78 us (13%)
  other arithmetic  3.02 us (4%)
  waiting for transfers between devices  1.58 us (2%)
  between operations  0.94 us (1%)
    all_to_all x1, blocking collectives, per_device(): lax.all_to_all(rows, 'head', split_axis=0, concat_axis=0, tiled=True)  29.1 us
    ppermute x4, starting transfers between devices, per_device(): lax.ppermute(m.astype(jnp.float16), 'ctx', fan(hop)).astype(f32)  10.1 us
    unnamed x50, local copies, waits for them, and re-layouts  9.78 us
    pallas_call x2, Pallas kernels, local(): call(functools.partial(local_kernel, parts), outs, [IN_VMEM] * 8 + [IN_SM...  9.18 us
    pallas_call x1, Pallas kernels, per_device(): call(sums_kernel, (pltpu.VMEM((2 * STATE + 8, FEATS), f32), wide, wide, w...  4.62 us
    ppermute x1, starting transfers between devices, per_device(): other = lax.ppermute(own, 'ctx', swap)  3.33 us
    pallas_call x1, Pallas kernels, per_device(): call(finish_kernel, jax.ShapeDtypeStruct((length, FEATS + 2 * STATE), bf1...  3.28 us
    convert_element_type x4, other arithmetic, per_device(): lax.ppermute(m.astype(jnp.float16), 'ctx', fan(hop)).astype(f32)  2.94 us
  transfers between devices with their start and end apart: 9, of which 1 were waited for; matrix products, arithmetic and copies ran while one was open for 3% of the time, Pallas kernels for 12%

profile of v2, /device:TPU:1, one launch (start us, length us, event | category | flops | bytes accessed | tf_op | source)
XLA Modules:
  0.0 77.4 jit_solution(12794103563861159492)
XLA Ops:
  0.6 4.6 %shard_map.103 = (f32[264,512]{1,0:T(8,128)S(1)}, bf16[1024,512]{1,0:T(8,128)(2,1)S(1)}, bf16[1024,512]{1,0:T(8,128)(2,1)S(1)}, bf16[1024,512]{1,0:T(8,128)(2,1)...) custom-call(bf16[1024,512]{1,0:T(8,128)(2,1)} %u_hbm.1, ...), custom_call_target="tpu_custom_call" | custom-call | flops 1073741824 | bytes 1048576 | tf_op jit(solution)/shard_map/pallas_call | solution.py:363
  5.3 3.3 %collective-permute-start = (f32[264,512]{1,0:T(8,128)S(1)}, f32[264,512]{1,0:T(8,128)S(1)}, u32[]{:S(2)}, u32[]{:S(2)}) collective-permute-start(f32[264,512]{1,0:T(8,128)S(1)} %get-tuple-element.29.own_ref), channel_id=1, source_target_pairs={{0,16},{16,0},{32,48},{48,32},{64,80},{80,64},{96,112},{112,96},{1... | collective-permute-start | bytes 1622024 | tf_op jit(solution)/shard_map/ppermute | solution.py:392
  8.7 1.6 %collective-permute-done.other_ref = f32[264,512]{1,0:T(8,128)S(1)} collective-permute-done((f32[264,512]{1,0:T(8,128)S(1)}, f32[264,512]{1,0:T(8,128)S(1)}, u32[]{:S(2)}, u32[]{:S(2)}) %collective-permute-start) | collective-permute-done | bytes 540704 | tf_op jit(solution)/shard_map/ppermute | solution.py:392
  10.5 5.3 %collective-permute-start.4 = (f16[144,256]{1,0:T(8,128)(2,1)S(1)}, f16[144,256]{1,0:T(8,128)(2,1)S(1)}, u32[]{:S(2)}, u32[]{:S(2)}) collective-permute-start(f16[144,256]{1,0:T(8,128)(2,1)S(1)} %convert_element_type.30), channel_id=1, source_target_pairs={{0,128},{32,160},{64,192},{96,224},{128,0},{160,32},{192,64},{224,... | collective-permute-start | bytes 221192 | tf_op jit(solution)/shard_map/ppermute | solution.py:402
  15.9 4.0 %collective-permute-start.2 = (f16[144,512]{1,0:T(8,128)(2,1)S(1)}, f16[144,512]{1,0:T(8,128)(2,1)S(1)}, u32[]{:S(2)}, u32[]{:S(2)}) collective-permute-start(f16[144,512]{1,0:T(8,128)(2,1)S(1)} %convert_element_type.26), channel_id=1, source_target_pairs={{0,64},{32,96},{64,128},{96,160},{128,192},{160,224},{192,0},{224,... | collective-permute-start | bytes 442376 | tf_op jit(solution)/shard_map/ppermute | solution.py:402
  20.0 0.7 collective-permute-start.1
  20.7 6.1 %shard_map.105 = (f32[512,512]{1,0:T(8,128)S(1)}, f32[512,512]{1,0:T(8,128)S(1)}, f32[512,128]{1,0:T(8,128)S(1)}, f32[1024,128]{1,0:T(8,128)S(1)}, f32[128,512]{1,0:T(8,128)S(1)}) custom-call(bf16[1024,512]{1,0:T(8,128)(2,1)S(1)} %get-tuple-element.34.refs_0_.xdh_ref, bf16[1024,512]{1,0:T(8,128)(2,1)S(1)} %get-tuple-element.35.refs_1_.xdl_ref, ...), custom_call_target="tpu_custom_call" | custom-call | flops 4294967296 | bytes 1048576 | tf_op jit(solution)/shard_map/pallas_call | solution.py:413
  26.8 1.0 %copy-done.8 = f32[512,512]{1,0:T(8,128)} copy-done((f32[512,512]{1,0:T(8,128)}, f32[512,512]{1,0:T(8,128)S(1)}, u32[]{:S(2)}) %copy-start.8) | copy-done | bytes 1048600
  27.8 1.0 %copy-done.10 = f32[512,512]{1,0:T(8,128)} copy-done((f32[512,512]{1,0:T(8,128)}, f32[512,512]{1,0:T(8,128)S(1)}, u32[]{:S(2)}) %copy-start.10) | copy-done | bytes 1048600
  28.7 0.7 copy-done.12
  29.4 0.8 %copy-done.14 = f32[1024,128]{1,0:T(8,128)} copy-done((f32[1024,128]{1,0:T(8,128)}, f32[1024,128]{1,0:T(8,128)S(1)}, u32[]{:S(2)}) %copy-start.14) | copy-done | bytes 524312
  30.2 0.7 copy-done.16
  31.6 0.8 convert_element_type.29.refs_2_
  32.4 0.8 convert_element_type.27.refs_1_
  33.1 0.8 convert_element_type.25.refs_0_
  35.0 1.2 %copy-done.5 = bf16[1024,512]{1,0:T(8,128)(2,1)S(1)} copy-done((bf16[1024,512]{1,0:T(8,128)(2,1)S(1)}, bf16[1024,512]{1,0:T(8,128)(2,1)}, u32[]{:S(2)}) %copy-start.5) | copy-done | bytes 1048600
  36.2 1.2 %copy-done.7 = bf16[1024,512]{1,0:T(8,128)(2,1)S(1)} copy-done((bf16[1024,512]{1,0:T(8,128)(2,1)S(1)}, bf16[1024,512]{1,0:T(8,128)(2,1)}, u32[]{:S(2)}) %copy-start.7) | copy-done | bytes 1048600
  37.5 1.2 %copy-done.19 = bf16[1024,512]{1,0:T(8,128)(2,1)S(1)} copy-done((bf16[1024,512]{1,0:T(8,128)(2,1)S(1)}, bf16[1024,512]{1,0:T(8,128)(2,1)}, u32[]{:S(2)}) %copy-start.19) | copy-done | bytes 1048600
  38.7 0.9 %copy-done.21 = f32[8,64,128]{2,1,0:T(8,128)S(1)} copy-done((f32[8,64,128]{2,1,0:T(8,128)S(1)}, f32[8,64,128]{2,1,0:T(8,128)}, u32[]{:S(2)}) %copy-start.21) | copy-done | bytes 262168
  39.6 0.9 %copy-done.23 = bf16[1024,128]{1,0:T(8,128)(2,1)S(1)} copy-done((bf16[1024,128]{1,0:T(8,128)(2,1)S(1)}, bf16[1024,128]{1,0:T(8,128)(2,1)}, u32[]{:S(2)}) %copy-start.23) | copy-done | bytes 262168
  40.6 3.1 %shard_map.107 = (f32[512,512]{1,0:T(8,128)S(1)}, f32[512,512]{1,0:T(8,128)S(1)}, f32[512,128]{1,0:T(8,128)S(1)}, f32[512,128]{1,0:T(8,128)S(1)}) custom-call(bf16[1024,512]{1,0:T(8,128)(2,1)S(1)} %get-tuple-element.34.refs_0_.xdh_ref, bf16[1024,512]{1,0:T(8,128)(2,1)S(1)} %get-tuple-element.35.refs_1_.xdl_ref, bf16[1024,512]{1,0:T(8,128)(2,1)S(1)} %copy-done.5, ...), custom_call_target="tpu_custom_call" | custom-call | flops 2147483648 | bytes 1048576 | tf_op jit(solution)/shard_map/pallas_call | solution.py:413
  43.9 3.3 %shard_map.108 = bf16[1024,768]{1,0:T(8,128)(2,1)} custom-call(f32[264,512]{1,0:T(8,128)S(1)} %get-tuple-element.29.own_ref, f32[264,512]{1,0:T(8,128)S(1)} %collective-permute-done.other_ref, f32[144,512]{1,0:T(8,128)S(1)} %copy-done.2, f32[144,512]{1,0:T(8,128)S(1)} %copy-done.1, f32[144,512]{1,0:T(8,128)S(1)} %copy-done, f32[144,256]{1,0:T(8,128)S(1)} %copy-done.3, ...), custom_call_target="tpu_custom_call" | custom-call | flops 1073741824 | bytes 1048576 | tf_op jit(solution)/shard_map/pallas_call | solution.py:429
  47.2 29.1 %all_to_all.11 = bf16[16,64,768]{2,1,0:T(8,128)(2,1)S(1)} all-to-all(bf16[16,64,768]{2,1,0:T(8,128)(2,1)} %bitcast.4), channel_id=1, replica_groups=mesh['ctx'=16,'head'=16] {'head'}, dimensions={0} | all-to-all | bytes 3145728 | tf_op jit(solution)/shard_map/all_to_all | solution.py:437
  76.3 1.1 %shard_map.109 = (bf16[64,8192]{1,0:T(8,128)(2,1)}, bf16[64,1024]{1,0:T(8,128)(2,1)}, bf16[64,1024]{1,0:T(8,128)(2,1)}) custom-call(bf16[1024,768]{1,0:T(8,128)(2,1)S(1)} %bitcast.3), custom_call_target="tpu_custom_call" | custom-call | bytes 1048576 | tf_op jit(solution)/shard_map/pallas_call | solution.py:439
  (60 shorter events, 2.3 us)
Async XLA Ops:
  5.3 21.5 %copy-start.4 = (bf16[1024,512]{1,0:T(8,128)(2,1)}, bf16[1024,512]{1,0:T(8,128)(2,1)S(1)}, u32[]{:S(2)}) copy-start(bf16[1024,512]{1,0:T(8,128)(2,1)S(1)} %get-tuple-element.36.refs_2_.xuh_ref) | copy-start | bytes 3145732
  5.3 21.5 %copy-start.6 = (bf16[1024,512]{1,0:T(8,128)(2,1)}, bf16[1024,512]{1,0:T(8,128)(2,1)S(1)}, u32[]{:S(2)}) copy-start(bf16[1024,512]{1,0:T(8,128)(2,1)S(1)} %get-tuple-element.37.refs_3_.xul_ref) | copy-start | bytes 3145732
  5.3 21.5 %copy-start.18 = (bf16[1024,512]{1,0:T(8,128)(2,1)}, bf16[1024,512]{1,0:T(8,128)(2,1)S(1)}, u32[]{:S(2)}) copy-start(bf16[1024,512]{1,0:T(8,128)(2,1)S(1)} %get-tuple-element.38.refs_4_) | copy-start | bytes 3145732
  5.3 21.5 %copy-start.22 = (bf16[1024,128]{1,0:T(8,128)(2,1)}, bf16[1024,128]{1,0:T(8,128)(2,1)S(1)}, u32[]{:S(2)}) copy-start(bf16[1024,128]{1,0:T(8,128)(2,1)S(1)} %get-tuple-element.40.refs_6_) | copy-start | bytes 786436
  5.3 15.4 %copy-start.20 = (f32[8,64,128]{2,1,0:T(8,128)S(1)}, f32[8,64,128]{2,1,0:T(8,128)}, u32[]{:S(2)}) copy-start(f32[8,64,128]{2,1,0:T(8,128)} %refs_9_.3) | copy-start | bytes 786436
  5.3 15.4 %copy-start.24 = (f32[8]{0:T(128)S(1)}, f32[8]{0:T(128)}, u32[]{:S(2)}) copy-start(f32[8]{0:T(128)} %refs_8_.3) | copy-start | bytes 100
  5.3 4.9 %collective-permute-start = (f32[264,512]{1,0:T(8,128)S(1)}, f32[264,512]{1,0:T(8,128)S(1)}, u32[]{:S(2)}, u32[]{:S(2)}) collective-permute-start(f32[264,512]{1,0:T(8,128)S(1)} %get-tuple-element.29.own_ref), channel_id=1, source_target_pairs={{0,16},{16,0},{32,48},{48,32},{64,80},{80,64},{96,112},{112,96},{1... | collective-permute-start | bytes 1622024 | tf_op jit(solution)/shard_map/ppermute | solution.py:392
  10.5 20.4 %collective-permute-start.4 = (f16[144,256]{1,0:T(8,128)(2,1)S(1)}, f16[144,256]{1,0:T(8,128)(2,1)S(1)}, u32[]{:S(2)}, u32[]{:S(2)}) collective-permute-start(f16[144,256]{1,0:T(8,128)(2,1)S(1)} %convert_element_type.30), channel_id=1, source_target_pairs={{0,128},{32,160},{64,192},{96,224},{128,0},{160,32},{192,64},{224,... | collective-permute-start | bytes 221192 | tf_op jit(solution)/shard_map/ppermute | solution.py:402
  15.8 15.8 %collective-permute-start.3 = (f16[144,512]{1,0:T(8,128)(2,1)S(1)}, f16[144,512]{1,0:T(8,128)(2,1)S(1)}, u32[]{:S(2)}, u32[]{:S(2)}) collective-permute-start(f16[144,512]{1,0:T(8,128)(2,1)S(1)} %convert_element_type.28), channel_id=1, source_target_pairs={{0,96},{32,128},{64,160},{96,192},{128,224},{160,0},{192,32},{224,... | collective-permute-start | bytes 442376 | tf_op jit(solution)/shard_map/ppermute | solution.py:402
  15.9 16.4 %collective-permute-start.2 = (f16[144,512]{1,0:T(8,128)(2,1)S(1)}, f16[144,512]{1,0:T(8,128)(2,1)S(1)}, u32[]{:S(2)}, u32[]{:S(2)}) collective-permute-start(f16[144,512]{1,0:T(8,128)(2,1)S(1)} %convert_element_type.26), channel_id=1, source_target_pairs={{0,64},{32,96},{64,128},{96,160},{128,192},{160,224},{192,0},{224,... | collective-permute-start | bytes 442376 | tf_op jit(solution)/shard_map/ppermute | solution.py:402
  20.0 13.2 %collective-permute-start.1 = (f16[144,512]{1,0:T(8,128)(2,1)S(1)}, f16[144,512]{1,0:T(8,128)(2,1)S(1)}, u32[]{:S(2)}, u32[]{:S(2)}) collective-permute-start(f16[144,512]{1,0:T(8,128)(2,1)S(1)} %convert_element_type.24), channel_id=1, source_target_pairs={{0,32},{32,64},{64,96},{96,128},{128,160},{160,192},{192,224},{224... | collective-permute-start | bytes 442376 | tf_op jit(solution)/shard_map/ppermute | solution.py:402
  33.9 9.9 %collective-permute-start.5 = (f32[144,512]{1,0:T(8,128)}, f32[144,512]{1,0:T(8,128)S(1)}, u32[]{:S(2)}, u32[]{:S(2)}) collective-permute-start(f32[144,512]{1,0:T(8,128)} %get-tuple-element.43.a_ref), channel_id=1, source_target_pairs={{0,16},{16,0},{32,48},{48,32},{64,80},{80,64},{96,112},{112,96},{1... | collective-permute-start | bytes 884744 | tf_op jit(solution)/shard_map/ppermute | solution.py:427
  33.9 9.9 %collective-permute-start.6 = (f32[144,512]{1,0:T(8,128)}, f32[144,512]{1,0:T(8,128)S(1)}, u32[]{:S(2)}, u32[]{:S(2)}) collective-permute-start(f32[144,512]{1,0:T(8,128)} %get-tuple-element.44.b_ref), channel_id=1, source_target_pairs={{0,16},{16,0},{32,48},{48,32},{64,80},{80,64},{96,112},{112,96},{1... | collective-permute-start | bytes 884744 | tf_op jit(solution)/shard_map/ppermute | solution.py:427
  34.4 9.4 %collective-permute-start.7 = (f32[144,512]{1,0:T(8,128)}, f32[144,512]{1,0:T(8,128)S(1)}, u32[]{:S(2)}, u32[]{:S(2)}) collective-permute-start(f32[144,512]{1,0:T(8,128)} %get-tuple-element.45.c_ref), channel_id=1, source_target_pairs={{0,16},{16,0},{32,48},{48,32},{64,80},{80,64},{96,112},{112,96},{1... | collective-permute-start | bytes 884744 | tf_op jit(solution)/shard_map/ppermute | solution.py:427
  34.4 9.4 %copy-start = (f32[144,512]{1,0:T(8,128)S(1)}, f32[144,512]{1,0:T(8,128)}, u32[]{:S(2)}) copy-start(f32[144,512]{1,0:T(8,128)} %get-tuple-element.45.c_ref) | copy-start | bytes 884740
  34.4 9.4 %copy-start.1 = (f32[144,512]{1,0:T(8,128)S(1)}, f32[144,512]{1,0:T(8,128)}, u32[]{:S(2)}) copy-start(f32[144,512]{1,0:T(8,128)} %get-tuple-element.44.b_ref) | copy-start | bytes 884740
  34.4 9.4 %copy-start.2 = (f32[144,512]{1,0:T(8,128)S(1)}, f32[144,512]{1,0:T(8,128)}, u32[]{:S(2)}) copy-start(f32[144,512]{1,0:T(8,128)} %get-tuple-element.43.a_ref) | copy-start | bytes 884740
  34.4 9.4 %copy-start.3 = (f32[144,256]{1,0:T(8,128)S(1)}, f32[144,256]{1,0:T(8,128)}, u32[]{:S(2)}) copy-start(f32[144,256]{1,0:T(8,128)} %get-tuple-element.46.far_ref) | copy-start | bytes 442372
  34.4 9.3 %collective-permute-start.8 = (f32[144,256]{1,0:T(8,128)}, f32[144,256]{1,0:T(8,128)S(1)}, u32[]{:S(2)}, u32[]{:S(2)}) collective-permute-start(f32[144,256]{1,0:T(8,128)} %get-tuple-element.46.far_ref), channel_id=1, source_target_pairs={{0,16},{16,0},{32,48},{48,32},{64,80},{80,64},{96,112},{112,96},{1... | collective-permute-start | bytes 442376 | tf_op jit(solution)/shard_map/ppermute | solution.py:427
  40.6 3.2 %copy-start.9 = (f32[512,512]{1,0:T(8,128)S(1)}, f32[512,512]{1,0:T(8,128)}, u32[]{:S(2)}) copy-start(f32[512,512]{1,0:T(8,128)} %copy-done.8) | copy-start | bytes 3145732
  40.6 3.2 %copy-start.11 = (f32[512,512]{1,0:T(8,128)S(1)}, f32[512,512]{1,0:T(8,128)}, u32[]{:S(2)}) copy-start(f32[512,512]{1,0:T(8,128)} %copy-done.10) | copy-start | bytes 3145732
  40.6 3.3 %copy-start.13 = (f32[512,128]{1,0:T(8,128)S(1)}, f32[512,128]{1,0:T(8,128)}, u32[]{:S(2)}) copy-start(f32[512,128]{1,0:T(8,128)} %copy-done.12) | copy-start | bytes 786436
  40.6 3.3 %copy-start.15 = (f32[1024,128]{1,0:T(8,128)S(1)}, f32[1024,128]{1,0:T(8,128)}, u32[]{:S(2)}) copy-start(f32[1024,128]{1,0:T(8,128)} %copy-done.14) | copy-start | bytes 1572868
  40.6 3.3 %copy-start.17 = (f32[128,512]{1,0:T(8,128)S(1)}, f32[128,512]{1,0:T(8,128)}, u32[]{:S(2)}) copy-start(f32[128,512]{1,0:T(8,128)} %copy-done.16) | copy-start | bytes 786436
  (10 other events, 9.7 us)

commit v3 on v2

v3 whole, which is shorter than its diff:
```python
import functools

import jax
import jax.numpy as jnp
from jax import lax
from jax.experimental import pallas as pl
from jax.experimental.pallas import tpu as pltpu
from jax.sharding import PartitionSpec as P

HEADS = 128
HEAD_SIZE = 64
STATE = 128
GROUPS = 8
TOKENS_DEV = 1024
HEADS_DEV = 8
FEATS = HEADS_DEV * HEAD_SIZE
CHUNK = 256
CHUNKS = TOKENS_DEV // CHUNK
CHIPS = 8
FAR = CHIPS // 2
ROWS = STATE + 8
LEAST = 1e-30

f32 = jnp.float32
bf16 = jnp.bfloat16
VMEM_LIMIT = 12 * 1024 * 1024


def nn(a, b):
    return lax.dot_general(a, b, (((1,), (0,)), ((), ())), preferred_element_type=f32)


def nt(a, b):
    return lax.dot_general(a, b, (((1,), (1,)), ((), ())), preferred_element_type=f32)


def tn(a, b):
    return lax.dot_general(a, b, (((0,), (0,)), ((), ())), preferred_element_type=f32)


def halves(x):
    high = x.astype(bf16)
    return high, (x - high.astype(f32)).astype(bf16)


def parts_of(x):
    high = x.astype(bf16).astype(f32)
    mid = (x - high).astype(bf16).astype(f32)
    return [high, mid, x - high - mid]


def head_columns():
    row = lax.broadcasted_iota(jnp.int32, (3 * HEADS_DEV, FEATS), 0) % HEADS_DEV
    col = lax.broadcasted_iota(jnp.int32, (3 * HEADS_DEV, FEATS), 1) // HEAD_SIZE
    return jnp.where(row == col, 1.0, 0.0).astype(bf16)


def spread(per_head, columns):
    high = per_head.astype(bf16).astype(f32)
    rest = per_head - high
    mid = rest.astype(bf16).astype(f32)
    low = rest - mid
    return tn(jnp.concatenate([high, mid, low], axis=0).astype(bf16), columns)


def head_vector(ref):
    row = lax.broadcasted_iota(jnp.int32, (HEADS_DEV, STATE), 0)
    out = jnp.zeros((HEADS_DEV, STATE), f32)
    for h in range(HEADS_DEV):
        out = jnp.where(row == h, ref[h], out)
    return out


def cumulate(x):
    width = 128
    runs = x.shape[1] // width
    stacked = jnp.concatenate([x[:, k * width : (k + 1) * width] for k in range(runs)], axis=0)
    row = lax.broadcasted_iota(jnp.int32, (width, width), 0)
    col = lax.broadcasted_iota(jnp.int32, (width, width), 1)
    ones = jnp.where(row <= col, 1.0, 0.0).astype(bf16)
    parts = jnp.concatenate(parts_of(stacked), axis=1).astype(bf16)
    inner = nn(parts, jnp.concatenate([ones] * 3, axis=0))
    out, offset = [], jnp.zeros((HEADS_DEV, width), f32)
    for k in range(runs):
        run = inner[k * HEADS_DEV : (k + 1) * HEADS_DEV]
        out.append(run + offset)
        offset = offset + jnp.broadcast_to(run[:, width - 1 :], (HEADS_DEV, width))
    return jnp.concatenate(out, axis=1)


def rows_of(i):
    return pl.ds(i * CHUNK if isinstance(i, int) else pl.multiple_of(i * CHUNK, CHUNK), CHUNK)


def slot(i):
    return pl.ds(i * STATE if isinstance(i, int) else pl.multiple_of(i * STATE, STATE), STATE)


def sums_kernel(
    u_hbm, dy_hbm, w_hbm, r_hbm, step_hbm, rate_hbm,
    out_ref, xdh_ref, xdl_ref, xuh_ref, xul_ref, dy_ref, w_ref, r_ref, bt_ref, early_ref, late_ref,
    u_ref, at_ref, step_ref, rate_ref, sems,
):
    column = pl.multiple_of(lax.axis_index("head") // 2 * STATE, STATE)
    small = [
        pltpu.make_async_copy(step_hbm, step_ref, sems.at[CHUNKS, 0]),
        pltpu.make_async_copy(rate_hbm, rate_ref, sems.at[CHUNKS, 1]),
    ]
    for copy in small:
        copy.start()

    def copies(k):
        rows, back = rows_of(k), rows_of(CHUNKS - 1 - k)
        return [
            pltpu.make_async_copy(u_hbm.at[rows, :], u_ref.at[rows, :], sems.at[k, 0]),
            pltpu.make_async_copy(w_hbm.at[rows, pl.ds(column, STATE)], w_ref.at[rows, :], sems.at[k, 1]),
            pltpu.make_async_copy(dy_hbm.at[back, :], dy_ref.at[back, :], sems.at[k, 2]),
            pltpu.make_async_copy(r_hbm.at[back, pl.ds(column, STATE)], r_ref.at[back, :], sems.at[k, 3]),
        ]

    for k in range(CHUNKS):
        for copy in copies(k):
            copy.start()
    columns = head_columns()
    for copy in small:
        copy.wait()
    steps = step_ref[...]
    rate = head_vector(rate_ref)[:, :1]
    cum = cumulate(-steps * rate)
    last = cum[:, TOKENS_DEV - 1 :]
    middle = 0.5 * last
    ahead = jnp.exp(cum - middle)
    at_ref[...] = ahead
    bt_ref[...] = jnp.exp(middle - cum) * steps
    wide = lambda x: spread(jnp.broadcast_to(x, (HEADS_DEV, STATE)), columns)
    half = wide(jnp.exp(middle))
    early_ref[pl.ds(0, STATE), :] = jnp.zeros((STATE, FEATS), f32)
    late_ref[pl.ds(CHUNKS * STATE, STATE), :] = jnp.zeros((STATE, FEATS), f32)

    def weigh(per_head_ref, i, values, high_ref, low_ref, vectors):
        rows = rows_of(i)
        weights = spread(per_head_ref[:, rows], columns)
        high, low = halves(weights * values[rows, :].astype(f32))
        high_ref[rows, :] = high
        low_ref[rows, :] = low
        both = tn(vectors[rows, :], jnp.concatenate([high, low], axis=1))
        return both[:, :FEATS] + both[:, FEATS:]

    def step(k):
        for copy in copies(k):
            copy.wait()
        early_ref[slot(k + 1), :] = early_ref[slot(k), :] + weigh(bt_ref, k, u_ref, xuh_ref, xul_ref, w_ref)
        i = CHUNKS - 1 - k
        late_ref[slot(i), :] = late_ref[slot(i + 1), :] + weigh(at_ref, i, dy_ref, xdh_ref, xdl_ref, r_ref)

    for k in range(CHUNKS):
        step(k)
    out_ref[pl.ds(0, STATE), :] = half * early_ref[slot(CHUNKS), :]
    out_ref[pl.ds(STATE, STATE), :] = half * late_ref[slot(0), :]
    out_ref[pl.ds(2 * STATE, 8), :] = wide(last)[:8, :]


def message_kernel(own_ref, other_ref, a_ref, b_ref, c_ref, far_ref, w_ref, r_ref):
    place = lax.axis_index("ctx")
    chip, core = place // 2, place % 2
    own_log = own_ref[pl.ds(2 * STATE, 1), :]
    other_log = other_ref[pl.ds(2 * STATE, 1), :]
    own_decay = jnp.exp(own_log)
    other_decay = jnp.exp(other_log)
    first = core == 0
    one = jnp.ones_like(own_decay)
    logs = parts_of(own_log + other_log)
    for ref, left, right, at in (
        (w_ref, jnp.where(first, other_decay, one), jnp.where(first, one, own_decay), 0),
        (r_ref, jnp.where(first, one, other_decay), jnp.where(first, own_decay, one), STATE),
    ):
        rows = pl.ds(at, STATE)
        total = left * own_ref[rows, :] + right * other_ref[rows, :]
        scale = jnp.maximum(jnp.max(jnp.abs(total), axis=0, keepdims=True), LEAST)
        ref[pl.ds(0, STATE), :] = total * (1.0 / scale)
        ref[pl.ds(STATE, 8), :] = jnp.concatenate(
            logs + parts_of(jnp.log(scale)) + [jnp.zeros((2, FEATS), f32)], axis=0
        )
    for hop, ref in ((1, a_ref), (2, b_ref), (3, c_ref)):
        to_later = jnp.where(first, chip + hop < CHIPS, chip - hop < 0)

        @pl.when(to_later)
        def _():
            ref[...] = w_ref[...]

        @pl.when(jnp.logical_not(to_later))
        def _():
            ref[...] = r_ref[...]

    half = FEATS // 2
    later = chip < FAR
    for part in range(2):
        cols = pl.ds(part * half, half)

        @pl.when(jnp.logical_and(later, core == part))
        def _():
            far_ref[...] = w_ref[:, cols]

        @pl.when(jnp.logical_and(jnp.logical_not(later), core == part))
        def _():
            far_ref[...] = r_ref[:, cols]


def local_kernel(
    xdh_ref, xdl_ref, xuh_ref, xul_ref, dy_ref, w_ref, r_ref, bt_ref, skip_ref, init_ref,
    gi_ref, back_ref, pw_ref, pr_ref, init_t_ref,
):
    columns = head_columns()
    skip = spread(head_vector(skip_ref), columns)[:1, :]
    init_t_ref[...] = init_ref[...].reshape(FEATS, STATE).T
    row = lax.broadcasted_iota(jnp.int32, (CHUNK, CHUNK), 0)
    col = lax.broadcasted_iota(jnp.int32, (CHUNK, CHUNK), 1)
    keep = col >= row
    for i in range(CHUNKS):
        rows = rows_of(i)
        writes, reads = w_ref[rows, :], r_ref[rows, :]
        uh, ul = xuh_ref[rows, :], xul_ref[rows, :]
        dh, dl = xdh_ref[rows, :], xdl_ref[rows, :]
        pairs = nt(jnp.concatenate([uh, uh, ul], axis=1), jnp.concatenate([dh, dl, dh], axis=1))
        ph, plow = halves(jnp.where(keep, pairs, 0.0))
        gh, gl = halves(jnp.where(keep, nt(writes, reads), 0.0))
        total = nn(jnp.concatenate([gh, gh, gl], axis=1), jnp.concatenate([dh, dl, dh], axis=0))
        back = spread(bt_ref[:, i * CHUNK : (i + 1) * CHUNK], columns)
        back_ref[rows, :] = back
        gi_ref[rows, :] = back * total + skip * dy_ref[rows, :].astype(f32)
        pw_ref[rows, :] = nn(ph, reads) + nn(plow, reads)
        pr_ref[rows, :] = tn(ph, writes) + tn(plow, writes)


def finish_kernel(
    own_ref, other_ref, a_ref, b_ref, c_ref, far_ref, oa_ref, ob_ref, oc_ref, ofar_ref,
    xdh_ref, xdl_ref, xuh_ref, xul_ref, w_ref, early_ref, late_ref,
    gi_ref, back_ref, pw_ref, pr_ref, init_t_ref,
    rows_ref, s_ref, t_ref, states_ref, adjoints_ref,
):
    place = lax.axis_index("ctx")
    chip, core = place // 2, place % 2
    first = core == 0
    mine, theirs = (a_ref, b_ref, c_ref), (oa_ref, ob_ref, oc_ref)

    logs_at = pl.ds(STATE, 8)

    def logs(rows):
        return rows[0:1] + rows[1:2] + rows[2:3], rows[3:4] + rows[4:5] + rows[5:6]

    below, above = {}, {}
    for hop in range(1, FAR):
        own_rows, other_rows = mine[hop - 1][logs_at, :], theirs[hop - 1][logs_at, :]
        low, high = jnp.where(first, own_rows, other_rows), jnp.where(first, other_rows, own_rows)
        below[hop] = above[CHIPS - hop] = logs(low)
        above[hop] = below[CHIPS - hop] = logs(high)
    own_rows, other_rows = far_ref[logs_at, :], ofar_ref[logs_at, :]
    below[FAR] = above[FAR] = logs(
        jnp.concatenate(
            [jnp.where(first, own_rows, other_rows), jnp.where(first, other_rows, own_rows)], axis=1
        )
    )

    def weigh(table, inside):
        weights, total = {}, jnp.zeros((1, FEATS), f32)
        for hop in range(1, CHIPS):
            decay, scale = table[hop]
            weights[hop] = jnp.where(inside(hop), jnp.exp(total + scale), 0.0)
            total = total + jnp.where(inside(hop), decay, 0.0)
        return weights, total

    to_state, total = weigh(below, lambda hop: chip - hop >= 0)
    to_adjoint, _ = weigh(above, lambda hop: chip + hop < CHIPS)
    weight_init = jnp.exp(total)
    terms = []
    for hop in range(1, FAR):
        low = to_state[hop], to_adjoint[CHIPS - hop]
        high = to_state[CHIPS - hop], to_adjoint[hop]
        for ref, own in ((mine[hop - 1], True), (theirs[hop - 1], False)):
            one, two = (low, high) if own else (high, low)
            terms.append((ref, jnp.where(first, one[0], two[0]), jnp.where(first, one[1], two[1])))

    own_log = own_ref[pl.ds(2 * STATE, 1), :]
    other_decay = jnp.exp(other_ref[pl.ds(2 * STATE, 1), :])
    half = jnp.exp(0.5 * own_log)
    keep_s = jnp.where(first, half, half * other_decay)
    keep_a = jnp.where(first, half * other_decay, half)
    add_s = jnp.where(first, 0.0, half)
    add_a = jnp.where(first, half, 0.0)
    step = 32
    for at in range(0, STATE, step):
        rows = pl.ds(at, step)
        near, distant = far_ref[rows, :], ofar_ref[rows, :]
        middle = jnp.concatenate(
            [jnp.where(first, near, distant), jnp.where(first, distant, near)], axis=1
        )
        state = weight_init * init_t_ref[rows, :] + to_state[FAR] * middle
        adjoint = to_adjoint[FAR] * middle
        for ref, for_state, for_adjoint in terms:
            value = ref[rows, :]
            state = state + for_state * value
            adjoint = adjoint + for_adjoint * value
        states_ref[rows, :] = keep_s * state + add_s * other_ref[rows, :]
        adjoints_ref[rows, :] = keep_a * adjoint + add_a * other_ref[pl.ds(STATE + at, step), :]

    for i in range(CHUNKS):
        rows = rows_of(i)
        base = i * 2 * STATE
        state = states_ref[...] + early_ref[slot(i), :]
        adjoint = adjoints_ref[...] + late_ref[slot(i + 1), :]
        sh, sl = halves(state)
        th, tl = halves(adjoint)
        s_ref[pl.ds(base, STATE), :] = sh
        s_ref[pl.ds(base + STATE, STATE), :] = sl
        t_ref[pl.ds(base, STATE), :] = th
        t_ref[pl.ds(base + STATE, STATE), :] = tl
        both, high = pl.ds(base, 2 * STATE), pl.ds(base, STATE)
        reads = nt(xdh_ref[rows, :], s_ref[both, :])
        reads = reads[:, :STATE] + reads[:, STATE:] + nt(xdl_ref[rows, :], s_ref[high, :])
        writes = nt(xuh_ref[rows, :], t_ref[both, :])
        writes = writes[:, :STATE] + writes[:, STATE:] + nt(xul_ref[rows, :], t_ref[high, :])
        vectors = w_ref[rows, :]
        through = nn(jnp.concatenate([vectors, vectors], axis=1), t_ref[both, :])
        rows_ref[rows, pl.ds(0, FEATS)] = (gi_ref[rows, :] + back_ref[rows, :] * through).astype(bf16)
        rows_ref[rows, pl.ds(FEATS, STATE)] = (pw_ref[rows, :] + writes).astype(bf16)
        rows_ref[rows, pl.ds(FEATS + STATE, STATE)] = (pr_ref[rows, :] + reads).astype(bf16)


def relay_kernel(*refs):
    pass


def arrange_kernel(in_ref, gi_hbm, gw_hbm, gr_hbm, gw_ref, gr_ref, sems):
    share = gw_ref.shape[0]
    peers = in_ref.shape[0] // share
    copies = []
    for j in range(peers):
        copies.append(
            pltpu.make_async_copy(
                in_ref.at[pl.ds(j * share, share), pl.ds(0, FEATS)],
                gi_hbm.at[:, pl.ds(j * FEATS, FEATS)],
                sems.at[j],
            )
        )
        copies[-1].start()
    for n, (ref, out, at) in enumerate(((gw_ref, gw_hbm, FEATS), (gr_ref, gr_hbm, FEATS + STATE))):
        cols = pl.ds(at, STATE)
        for g in range(GROUPS):
            one, two = pl.ds(2 * g * share, share), pl.ds((2 * g + 1) * share, share)
            ref[:, pl.ds(g * STATE, STATE)] = (
                in_ref[one, cols].astype(f32) + in_ref[two, cols].astype(f32)
            ).astype(bf16)
        copies.append(pltpu.make_async_copy(ref, out, sems.at[peers + n]))
        copies[-1].start()
    for copy in copies:
        copy.wait()


def call(body, outs, ins, scratch=(), flops=0, places=None):
    return pl.pallas_call(
        body,
        out_shape=outs,
        **({} if places is None else {"out_specs": places}),
        in_specs=ins,
        scratch_shapes=scratch,
        compiler_params=pltpu.CompilerParams(vmem_limit_bytes=VMEM_LIMIT),
        cost_estimate=pl.CostEstimate(flops=flops, bytes_accessed=1 << 20, transcendentals=0),
    )


IN_HBM = pl.BlockSpec(memory_space=pltpu.HBM)
IN_ANY = pl.BlockSpec(memory_space=pl.ANY)
IN_VMEM = pl.BlockSpec(memory_space=pltpu.VMEM)
IN_SMEM = pl.BlockSpec(memory_space=pltpu.SMEM)


def per_device(inputs, upstream, step_size, decay_rate, write_proj, read_proj, init_state, skip_gain):
    length = TOKENS_DEV
    wide = pltpu.VMEM((length, FEATS), bf16)
    wide32 = pltpu.VMEM((length, FEATS), f32)
    thin = pltpu.VMEM((length, STATE), bf16)
    thin32 = pltpu.VMEM((length, STATE), f32)
    parts = pltpu.VMEM(((CHUNKS + 1) * STATE, FEATS), f32)
    own, xdh, xdl, xuh, xul, dy, w, r, bt, early, late = call(
        sums_kernel,
        (
            pltpu.VMEM((2 * STATE + 8, FEATS), f32),
            wide, wide, wide, wide, wide, thin, thin,
            pltpu.VMEM((HEADS_DEV, length), f32),
            parts,
            parts,
        ),
        [IN_HBM] * 6,
        [
            pltpu.VMEM((length, FEATS), bf16),
            pltpu.VMEM((HEADS_DEV, length), f32),
            pltpu.VMEM((HEADS_DEV, length), f32),
            pltpu.SMEM((HEADS_DEV,), f32),
            pltpu.SemaphoreType.DMA((CHUNKS + 1, 4)),
        ],
        flops=1 << 30,
    )(
        *(
            pltpu.with_memory_space_constraint(a, pltpu.HBM)
            for a in (inputs, upstream, write_proj, read_proj, step_size.T, decay_rate)
        )
    )

    swap = [(i, i ^ 1) for i in range(2 * CHIPS)]

    def fan(hop):
        up = [(2 * z, 2 * ((z + hop) % CHIPS)) for z in range(CHIPS)]
        down = [(2 * z + 1, 2 * ((z - hop) % CHIPS) + 1) for z in range(CHIPS)]
        return up + down

    other = lax.ppermute(own, "ctx", swap)
    message = jax.ShapeDtypeStruct((ROWS, FEATS), f32)
    messages = call(
        message_kernel,
        (message, message, message, jax.ShapeDtypeStruct((ROWS, FEATS // 2), f32)),
        [IN_VMEM, IN_VMEM],
        [pltpu.VMEM((ROWS, FEATS), f32), pltpu.VMEM((ROWS, FEATS), f32)],
        flops=1 << 20,
    )(own, other)
    mine = [
        lax.ppermute(m.astype(jnp.float16), "ctx", fan(hop))
        for m, hop in zip(messages, (1, 2, 3, FAR))
    ]

    local = call(
        local_kernel,
        (wide32, wide32, thin32, thin32, pltpu.VMEM((STATE, FEATS), f32)),
        [IN_VMEM] * 8 + [IN_SMEM, IN_VMEM],
        flops=0,
    )(xdh, xdl, xuh, xul, dy, w, r, bt, skip_gain, init_state)
    def after(m, token):
        return lax.optimization_barrier((m, token))[0]

    near = mine[:3]
    far = after(mine[3], local[2])
    mine = [after(m, far) for m in near] + [far]
    theirs = [lax.ppermute(m, "ctx", swap).astype(f32) for m in mine]
    mine = [m.astype(f32) for m in mine]

    rows = call(
        finish_kernel,
        jax.ShapeDtypeStruct((length, FEATS + 2 * STATE), bf16),
        [IN_VMEM] * 22,
        [
            pltpu.VMEM((CHUNKS * 2 * STATE, FEATS), bf16),
            pltpu.VMEM((CHUNKS * 2 * STATE, FEATS), bf16),
            pltpu.VMEM((STATE, FEATS), f32),
            pltpu.VMEM((STATE, FEATS), f32),
        ],
        flops=1 << 30,
    )(own, other, *mine, *theirs, xdh, xdl, xuh, xul, w, early, late, *local)

    moved = lax.all_to_all(rows, "head", split_axis=0, concat_axis=0, tiled=True)
    share = length // lax.axis_size("head")
    return call(
        arrange_kernel,
        (
            jax.ShapeDtypeStruct((share, HEADS * HEAD_SIZE), bf16),
            jax.ShapeDtypeStruct((share, GROUPS * STATE), bf16),
            jax.ShapeDtypeStruct((share, GROUPS * STATE), bf16),
        ),
        [IN_VMEM],
        [
            pltpu.VMEM((share, GROUPS * STATE), bf16),
            pltpu.VMEM((share, GROUPS * STATE), bf16),
            pltpu.SemaphoreType.DMA((lax.axis_size("head") + 2,)),
        ],
        places=(IN_HBM,) * 3,
    )(moved)


def solution(mesh):
    placed = (
        P("ctx", "head"),
        P("ctx", "head"),
        P("ctx", "head"),
        P("head"),
        P("ctx", None),
        P("ctx", None),
        P("head", None, None),
        P("head"),
    )
    return jax.shard_map(
        per_device,
        mesh=mesh,
        in_specs=placed,
        out_specs=(P(("ctx", "head"), None), P(("ctx", "head"), None), P(("ctx", "head"), None)),
        check_vma=False,
    )
```

time: 77.7 us -> 65.4 us (0.84)
  local copies, waits for them, and re-layouts: 9.78 us -> 0.01 us
  Pallas kernels: 18.5 us -> 11.7 us
  waiting for transfers between devices: 1.58 us -> 6.08 us
  starting transfers between devices: 14.5 us -> 17.7 us
  other arithmetic: 3.02 us -> 0.23 us
    unnamed x50 -> x4, local copies, waits for them, and re-layouts: 9.78 us -> 0.01 us
    pallas_call x3 -> x1, Pallas kernels: 9.18 us -> 3.55 us  [per_device(): call(local_kernel, (wide32, wide32, thin32, thin32, pltpu.VMEM((STATE, FE...]
    ppermute x8, waiting for transfers between devices: 0.02 us -> 4.52 us  [the longest x4 3.37 us: per_device(): lax.ppermute(m.astype(jnp.float16), 'ctx', fan(hop))]
    ppermute x8, starting transfers between devices: 11.2 us -> 14.3 us  [the longest x4 10.3 us: per_device(): lax.ppermute(m.astype(jnp.float16), 'ctx', fan(hop))]
    convert_element_type x4 -> x8, other arithmetic: 2.94 us -> 0.16 us  [the longest x4 0.08 us: per_device(): mine = [m.astype(f32) for m in mine]]
    pallas_call x1, Pallas kernels: 3.28 us -> 1.97 us  [per_device(): call(finish_kernel, jax.ShapeDtypeStruct((length, FEATS + 2 * STATE), bf1...]
  transfers between devices with their start and end apart: 9 -> 9, of which waited for: 1 -> 4; matrix products, arithmetic and copies ran while one was open for 3% -> 0% of each run, Pallas kernels for 12% -> 5%
where the time goes in v3:
time: 65.4 us; the launch traced here: 65.2 us
  blocking collectives  28.7 us (44%)
  starting transfers between devices  17.7 us (27%)
  Pallas kernels  11.7 us (18%)
  waiting for transfers between devices  6.08 us (9%)
  between operations  0.94 us (1%)
    all_to_all x1, blocking collectives, per_device(): lax.all_to_all(rows, 'head', split_axis=0, concat_axis=0, tiled=True)  28.7 us
    ppermute x4, starting transfers between devices, per_device(): lax.ppermute(m.astype(jnp.float16), 'ctx', fan(hop))  10.3 us
    pallas_call x1, Pallas kernels, per_device(): call(sums_kernel, (pltpu.VMEM((2 * STATE + 8, FEATS), f32), wide, wide, w...  4.68 us
    ppermute x4, starting transfers between devices, per_device(): theirs = [lax.ppermute(m, 'ctx', swap).astype(f32) for m in mine]  4.07 us
    pallas_call x1, Pallas kernels, per_device(): call(local_kernel, (wide32, wide32, thin32, thin32, pltpu.VMEM((STATE, FE...  3.55 us
    ppermute x4, waiting for transfers between devices, per_device(): lax.ppermute(m.astype(jnp.float16), 'ctx', fan(hop))  3.37 us
    ppermute x1, starting transfers between devices, per_device(): other = lax.ppermute(own, 'ctx', swap)  3.32 us
    pallas_call x1, Pallas kernels, per_device(): call(finish_kernel, jax.ShapeDtypeStruct((length, FEATS + 2 * STATE), bf1...  1.97 us
  transfers between devices with their start and end apart: 9, of which 4 were waited for; matrix products, arithmetic and copies ran while one was open for 0% of the time, Pallas kernels for 5%

profile of v3, /device:TPU:1, one launch (start us, length us, event | category | flops | bytes accessed | tf_op | source)
XLA Modules:
  0.0 65.2 jit_solution(12380919478446591950)
XLA Ops:
  0.6 4.7 %shard_map.103 = (f32[264,512]{1,0:T(8,128)S(1)}, bf16[1024,512]{1,0:T(8,128)(2,1)S(1)}, bf16[1024,512]{1,0:T(8,128)(2,1)S(1)}, bf16[1024,512]{1,0:T(8,128)(2,1)...) custom-call(bf16[1024,512]{1,0:T(8,128)(2,1)} %u_hbm.1, ...), custom_call_target="tpu_custom_call" | custom-call | flops 1073741824 | bytes 1048576 | tf_op jit(solution)/shard_map/pallas_call | solution.py:384
  5.3 0.0 copy-start
  5.3 0.0 copy-start.1
  5.3 3.3 %collective-permute-start = (f32[264,512]{1,0:T(8,128)S(1)}, f32[264,512]{1,0:T(8,128)S(1)}, u32[]{:S(2)}, u32[]{:S(2)}) collective-permute-start(f32[264,512]{1,0:T(8,128)S(1)} %get-tuple-element.27.own_ref), channel_id=1, source_target_pairs={{0,16},{16,0},{32,48},{48,32},{64,80},{80,64},{96,112},{112,96},{1... | collective-permute-start | bytes 1622024 | tf_op jit(solution)/shard_map/ppermute | solution.py:416
  8.7 1.6 %collective-permute-done.other_ref = f32[264,512]{1,0:T(8,128)S(1)} collective-permute-done((f32[264,512]{1,0:T(8,128)S(1)}, f32[264,512]{1,0:T(8,128)S(1)}, u32[]{:S(2)}, u32[]{:S(2)}) %collective-permute-start) | collective-permute-done | bytes 540704 | tf_op jit(solution)/shard_map/ppermute | solution.py:416
  10.2 0.3 shard_map.104
  10.5 4.8 %collective-permute-start.4 = (f16[136,512]{1,0:T(8,128)(2,1)S(1)}, f16[136,512]{1,0:T(8,128)(2,1)S(1)}, u32[]{:S(2)}, u32[]{:S(2)}) collective-permute-start(f16[136,512]{1,0:T(8,128)(2,1)S(1)} %convert_element_type.41), channel_id=1, source_target_pairs={{0,96},{32,128},{64,160},{96,192},{128,224},{160,0},{192,32},{224,... | collective-permute-start | bytes 417800 | tf_op jit(solution)/shard_map/ppermute | solution.py:426
  15.4 0.3 collective-permute-start.3
  15.7 0.6 collective-permute-start.1
  16.3 4.6 %collective-permute-start.2 = (f16[136,256]{1,0:T(8,128)(2,1)S(1)}, f16[136,256]{1,0:T(8,128)(2,1)S(1)}, u32[]{:S(2)}, u32[]{:S(2)}) collective-permute-start(f16[136,256]{1,0:T(8,128)(2,1)S(1)} %convert_element_type.37), channel_id=1, source_target_pairs={{0,128},{32,160},{64,192},{96,224},{128,0},{160,32},{192,64},{224,... | collective-permute-start | bytes 208904 | tf_op jit(solution)/shard_map/ppermute | solution.py:426
  20.9 3.6 %shard_map.105 = (f32[1024,512]{1,0:T(8,128)S(1)}, f32[1024,512]{1,0:T(8,128)S(1)}, f32[1024,128]{1,0:T(8,128)S(1)}, f32[1024,128]{1,0:T(8,128)S(1)}, f32[128,512]{1,0:T(8,128)S(1)}) custom-call(bf16[1024,512]{1,0:T(8,128)(2,1)S(1)} %get-tuple-element.30.xdh_ref, bf16[1024,512]{1,0:T(8,128)(2,1)S(1)} %get-tuple-element.31.xdl_ref, ...), custom_call_target="tpu_custom_call" | custom-call | bytes 1048576 | tf_op jit(solution)/shard_map/pallas_call | solution.py:430
  24.4 1.7 %collective-permute-done.2 = f16[136,256]{1,0:T(8,128)(2,1)S(1)} collective-permute-done((f16[136,256]{1,0:T(8,128)(2,1)S(1)}, f16[136,256]{1,0:T(8,128)(2,1)S(1)}, u32[]{:S(2)}, u32[]{:S(2)}) %collective-permute-start.2) | collective-permute-done | bytes 69664 | tf_op jit(solution)/shard_map/ppermute | solution.py:426
  26.1 1.7 %collective-permute-done.1 = f16[136,512]{1,0:T(8,128)(2,1)S(1)} collective-permute-done((f16[136,512]{1,0:T(8,128)(2,1)S(1)}, f16[136,512]{1,0:T(8,128)(2,1)S(1)}, u32[]{:S(2)}, u32[]{:S(2)}) %collective-permute-start.1) | collective-permute-done | bytes 139296 | tf_op jit(solution)/shard_map/ppermute | solution.py:426
  27.8 3.5 %collective-permute-start.5 = (f16[136,512]{1,0:T(8,128)(2,1)S(1)}, f16[136,512]{1,0:T(8,128)(2,1)S(1)}, u32[]{:S(2)}, u32[]{:S(2)}) collective-permute-start(f16[136,512]{1,0:T(8,128)(2,1)S(1)} %collective-permute-done.1), channel_id=1, source_target_pairs={{0,16},{16,0},{32,48},{48,32},{64,80},{80,64},{96,112},{112,96},{1... | collective-permute-start | bytes 417800 | tf_op jit(solution)/shard_map/ppermute | solution.py:442
  31.2 0.1 collective-permute-start.6
  31.3 0.4 collective-permute-start.7
  31.8 0.1 collective-permute-start.8
  31.9 1.1 %collective-permute-done.8 = f16[136,256]{1,0:T(8,128)(2,1)S(1)} collective-permute-done((f16[136,256]{1,0:T(8,128)(2,1)S(1)}, f16[136,256]{1,0:T(8,128)(2,1)S(1)}, u32[]{:S(2)}, u32[]{:S(2)}) %collective-permute-start.8) | collective-permute-done | bytes 69664 | tf_op jit(solution)/shard_map/ppermute | solution.py:442
  33.1 0.0 collective-permute-done.5
  33.2 0.0 collective-permute-done.6
  33.2 0.0 collective-permute-done.7
  33.2 2.0 %shard_map.106 = bf16[1024,768]{1,0:T(8,128)(2,1)S(1)} custom-call(f32[264,512]{1,0:T(8,128)S(1)} %get-tuple-element.27.own_ref, f32[264,512]{1,0:T(8,128)S(1)} %collective-permute-done.other_ref, f32[136,512]{1,0:T(8,128)S(1)} %convert_element_type.38.a_ref, f32[136,512]{1,0:T(8,128)S(1)} %convert_element_type.40.b_ref, ...), custom_call_target="tpu_custom_call" | custom-call | flops 1073741824 | bytes 1048576 | tf_op jit(solution)/shard_map/pallas_call | solution.py:445
  35.2 28.7 %all_to_all.11 = bf16[16,64,768]{2,1,0:T(8,128)(2,1)S(1)} all-to-all(bf16[16,64,768]{2,1,0:T(8,128)(2,1)S(1)} %bitcast.3), channel_id=1, replica_groups=mesh['ctx'=16,'head'=16] {'head'}, dimensions={0} | all-to-all | bytes 3145728 | tf_op jit(solution)/shard_map/all_to_all | solution.py:458
  63.9 1.2 %shard_map.107 = (bf16[64,8192]{1,0:T(8,128)(2,1)}, bf16[64,1024]{1,0:T(8,128)(2,1)}, bf16[64,1024]{1,0:T(8,128)(2,1)}) custom-call(bf16[1024,768]{1,0:T(8,128)(2,1)S(1)} %bitcast.4), custom_call_target="tpu_custom_call" | custom-call | bytes 1048576 | tf_op jit(solution)/shard_map/pallas_call | solution.py:460
  (16 shorter events, 0.2 us)
Async XLA Ops:
  5.3 15.5 %copy-start = (f32[8,64,128]{2,1,0:T(8,128)S(1)}, f32[8,64,128]{2,1,0:T(8,128)}, u32[]{:S(2)}) copy-start(f32[8,64,128]{2,1,0:T(8,128)} %init_ref.1) | copy-start | bytes 786436
  5.3 15.5 %copy-start.1 = (f32[8]{0:T(128)S(1)}, f32[8]{0:T(128)}, u32[]{:S(2)}) copy-start(f32[8]{0:T(128)} %skip_ref.1) | copy-start | bytes 100
  5.3 4.9 %collective-permute-start = (f32[264,512]{1,0:T(8,128)S(1)}, f32[264,512]{1,0:T(8,128)S(1)}, u32[]{:S(2)}, u32[]{:S(2)}) collective-permute-start(f32[264,512]{1,0:T(8,128)S(1)} %get-tuple-element.27.own_ref), channel_id=1, source_target_pairs={{0,16},{16,0},{32,48},{48,32},{64,80},{80,64},{96,112},{112,96},{1... | collective-permute-start | bytes 1622024 | tf_op jit(solution)/shard_map/ppermute | solution.py:416
  10.5 15.6 %collective-permute-start.4 = (f16[136,512]{1,0:T(8,128)(2,1)S(1)}, f16[136,512]{1,0:T(8,128)(2,1)S(1)}, u32[]{:S(2)}, u32[]{:S(2)}) collective-permute-start(f16[136,512]{1,0:T(8,128)(2,1)S(1)} %convert_element_type.41), channel_id=1, source_target_pairs={{0,96},{32,128},{64,160},{96,192},{128,224},{160,0},{192,32},{224,... | collective-permute-start | bytes 417800 | tf_op jit(solution)/shard_map/ppermute | solution.py:426
  15.4 10.7 %collective-permute-start.3 = (f16[136,512]{1,0:T(8,128)(2,1)S(1)}, f16[136,512]{1,0:T(8,128)(2,1)S(1)}, u32[]{:S(2)}, u32[]{:S(2)}) collective-permute-start(f16[136,512]{1,0:T(8,128)(2,1)S(1)} %convert_element_type.39), channel_id=1, source_target_pairs={{0,64},{32,96},{64,128},{96,160},{128,192},{160,224},{192,0},{224,... | collective-permute-start | bytes 417800 | tf_op jit(solution)/shard_map/ppermute | solution.py:426
  15.7 12.1 %collective-permute-start.1 = (f16[136,512]{1,0:T(8,128)(2,1)S(1)}, f16[136,512]{1,0:T(8,128)(2,1)S(1)}, u32[]{:S(2)}, u32[]{:S(2)}) collective-permute-start(f16[136,512]{1,0:T(8,128)(2,1)S(1)} %convert_element_type.36), channel_id=1, source_target_pairs={{0,32},{32,64},{64,96},{96,128},{128,160},{160,192},{192,224},{224... | collective-permute-start | bytes 417800 | tf_op jit(solution)/shard_map/ppermute | solution.py:426
  16.3 9.8 %collective-permute-start.2 = (f16[136,256]{1,0:T(8,128)(2,1)S(1)}, f16[136,256]{1,0:T(8,128)(2,1)S(1)}, u32[]{:S(2)}, u32[]{:S(2)}) collective-permute-start(f16[136,256]{1,0:T(8,128)(2,1)S(1)} %convert_element_type.37), channel_id=1, source_target_pairs={{0,128},{32,160},{64,192},{96,224},{128,0},{160,32},{192,64},{224,... | collective-permute-start | bytes 208904 | tf_op jit(solution)/shard_map/ppermute | solution.py:426
  27.8 5.3 %collective-permute-start.5 = (f16[136,512]{1,0:T(8,128)(2,1)S(1)}, f16[136,512]{1,0:T(8,128)(2,1)S(1)}, u32[]{:S(2)}, u32[]{:S(2)}) collective-permute-start(f16[136,512]{1,0:T(8,128)(2,1)S(1)} %collective-permute-done.1), channel_id=1, source_target_pairs={{0,16},{16,0},{32,48},{48,32},{64,80},{80,64},{96,112},{112,96},{1... | collective-permute-start | bytes 417800 | tf_op jit(solution)/shard_map/ppermute | solution.py:442
  31.2 1.9 %collective-permute-start.6 = (f16[136,512]{1,0:T(8,128)(2,1)S(1)}, f16[136,512]{1,0:T(8,128)(2,1)S(1)}, u32[]{:S(2)}, u32[]{:S(2)}) collective-permute-start(f16[136,512]{1,0:T(8,128)(2,1)S(1)} %collective-permute-done.3), channel_id=1, source_target_pairs={{0,16},{16,0},{32,48},{48,32},{64,80},{80,64},{96,112},{112,96},{1... | collective-permute-start | bytes 417800 | tf_op jit(solution)/shard_map/ppermute | solution.py:442
  31.3 1.9 %collective-permute-start.7 = (f16[136,512]{1,0:T(8,128)(2,1)S(1)}, f16[136,512]{1,0:T(8,128)(2,1)S(1)}, u32[]{:S(2)}, u32[]{:S(2)}) collective-permute-start(f16[136,512]{1,0:T(8,128)(2,1)S(1)} %collective-permute-done.4), channel_id=1, source_target_pairs={{0,16},{16,0},{32,48},{48,32},{64,80},{80,64},{96,112},{112,96},{1... | collective-permute-start | bytes 417800 | tf_op jit(solution)/shard_map/ppermute | solution.py:442
  31.8 1.3 %collective-permute-start.8 = (f16[136,256]{1,0:T(8,128)(2,1)S(1)}, f16[136,256]{1,0:T(8,128)(2,1)S(1)}, u32[]{:S(2)}, u32[]{:S(2)}) collective-permute-start(f16[136,256]{1,0:T(8,128)(2,1)S(1)} %collective-permute-done.2), channel_id=1, source_target_pairs={{0,16},{16,0},{32,48},{48,32},{64,80},{80,64},{96,112},{112,96},{1... | collective-permute-start | bytes 208904 | tf_op jit(solution)/shard_map/ppermute | solution.py:442

commit v4 on v3

--- a/solution.py
+++ b/solution.py
@@ -98,8 +98,8 @@
 
 def sums_kernel(
     u_hbm, dy_hbm, w_hbm, r_hbm, step_hbm, rate_hbm,
-    out_ref, xdh_ref, xdl_ref, xuh_ref, xul_ref, dy_ref, w_ref, r_ref, bt_ref, early_ref, late_ref,
-    u_ref, at_ref, step_ref, rate_ref, sems,
+    out_ref, xdh_ref, xdl_ref, xuh_ref, xul_ref, dy_ref, w_ref, r_ref, back_ref, early_ref, late_ref,
+    u_ref, ahead_ref, step_ref, rate_ref, sems,
 ):
     column = pl.multiple_of(lax.axis_index("head") // 2 * STATE, STATE)
     small = [
@@ -130,17 +130,19 @@
     last = cum[:, TOKENS_DEV - 1 :]
     middle = 0.5 * last
     ahead = jnp.exp(cum - middle)
-    at_ref[...] = ahead
-    bt_ref[...] = jnp.exp(middle - cum) * steps
+    behind = jnp.exp(middle - cum) * steps
     wide = lambda x: spread(jnp.broadcast_to(x, (HEADS_DEV, STATE)), columns)
     half = wide(jnp.exp(middle))
+    for i in range(CHUNKS):
+        lanes = slice(i * CHUNK, (i + 1) * CHUNK)
+        back_ref[rows_of(i), :] = spread(behind[:, lanes], columns)
+        ahead_ref[rows_of(i), :] = spread(ahead[:, lanes], columns)
     early_ref[pl.ds(0, STATE), :] = jnp.zeros((STATE, FEATS), f32)
     late_ref[pl.ds(CHUNKS * STATE, STATE), :] = jnp.zeros((STATE, FEATS), f32)
 
-    def weigh(per_head_ref, i, values, high_ref, low_ref, vectors):
+    def weigh(weights, i, values, high_ref, low_ref, vectors):
         rows = rows_of(i)
-        weights = spread(per_head_ref[:, rows], columns)
-        high, low = halves(weights * values[rows, :].astype(f32))
+        high, low = halves(weights[rows, :] * values[rows, :].astype(f32))
         high_ref[rows, :] = high
         low_ref[rows, :] = low
         both = tn(vectors[rows, :], jnp.concatenate([high, low], axis=1))
@@ -149,9 +151,9 @@
     def step(k):
         for copy in copies(k):
             copy.wait()
-        early_ref[slot(k + 1), :] = early_ref[slot(k), :] + weigh(bt_ref, k, u_ref, xuh_ref, xul_ref, w_ref)
+        early_ref[slot(k + 1), :] = early_ref[slot(k), :] + weigh(back_ref, k, u_ref, xuh_ref, xul_ref, w_ref)
         i = CHUNKS - 1 - k
-        late_ref[slot(i), :] = late_ref[slot(i + 1), :] + weigh(at_ref, i, dy_ref, xdh_ref, xdl_ref, r_ref)
+        late_ref[slot(i), :] = late_ref[slot(i + 1), :] + weigh(ahead_ref, i, dy_ref, xdh_ref, xdl_ref, r_ref)
 
     for k in range(CHUNKS):
         step(k)
@@ -207,8 +209,8 @@
 
 
 def local_kernel(
-    xdh_ref, xdl_ref, xuh_ref, xul_ref, dy_ref, w_ref, r_ref, bt_ref, skip_ref, init_ref,
-    gi_ref, back_ref, pw_ref, pr_ref, init_t_ref,
+    xdh_ref, xdl_ref, xuh_ref, xul_ref, dy_ref, w_ref, r_ref, back_ref, skip_ref, init_ref,
+    gi_ref, pw_ref, pr_ref, init_t_ref,
 ):
     columns = head_columns()
     skip = spread(head_vector(skip_ref), columns)[:1, :]
@@ -225,17 +227,15 @@
         ph, plow = halves(jnp.where(keep, pairs, 0.0))
         gh, gl = halves(jnp.where(keep, nt(writes, reads), 0.0))
         total = nn(jnp.concatenate([gh, gh, gl], axis=1), jnp.concatenate([dh, dl, dh], axis=0))
-        back = spread(bt_ref[:, i * CHUNK : (i + 1) * CHUNK], columns)
-        back_ref[rows, :] = back
-        gi_ref[rows, :] = back * total + skip * dy_ref[rows, :].astype(f32)
+        gi_ref[rows, :] = back_ref[rows, :] * total + skip * dy_ref[rows, :].astype(f32)
         pw_ref[rows, :] = nn(ph, reads) + nn(plow, reads)
         pr_ref[rows, :] = tn(ph, writes) + tn(plow, writes)
 
 
 def finish_kernel(
     own_ref, other_ref, a_ref, b_ref, c_ref, far_ref, oa_ref, ob_ref, oc_ref, ofar_ref,
-    xdh_ref, xdl_ref, xuh_ref, xul_ref, w_ref, early_ref, late_ref,
-    gi_ref, back_ref, pw_ref, pr_ref, init_t_ref,
+    xdh_ref, xdl_ref, xuh_ref, xul_ref, w_ref, early_ref, late_ref, back_ref,
+    gi_ref, pw_ref, pr_ref, init_t_ref,
     rows_ref, s_ref, t_ref, states_ref, adjoints_ref,
 ):
     place = lax.axis_index("ctx")
@@ -381,19 +381,19 @@
     thin = pltpu.VMEM((length, STATE), bf16)
     thin32 = pltpu.VMEM((length, STATE), f32)
     parts = pltpu.VMEM(((CHUNKS + 1) * STATE, FEATS), f32)
-    own, xdh, xdl, xuh, xul, dy, w, r, bt, early, late = call(
+    own, xdh, xdl, xuh, xul, dy, w, r, back, early, late = call(
         sums_kernel,
         (
             pltpu.VMEM((2 * STATE + 8, FEATS), f32),
             wide, wide, wide, wide, wide, thin, thin,
-            pltpu.VMEM((HEADS_DEV, length), f32),
+            wide32,
             parts,
             parts,
         ),
         [IN_HBM] * 6,
         [
             pltpu.VMEM((length, FEATS), bf16),
-            pltpu.VMEM((HEADS_DEV, length), f32),
+            pltpu.VMEM((length, FEATS), f32),
             pltpu.VMEM((HEADS_DEV, length), f32),
             pltpu.SMEM((HEADS_DEV,), f32),
             pltpu.SemaphoreType.DMA((CHUNKS + 1, 4)),
@@ -429,16 +429,15 @@
 
     local = call(
         local_kernel,
-        (wide32, wide32, thin32, thin32, pltpu.VMEM((STATE, FEATS), f32)),
+        (wide32, thin32, thin32, pltpu.VMEM((STATE, FEATS), f32)),
         [IN_VMEM] * 8 + [IN_SMEM, IN_VMEM],
         flops=0,
-    )(xdh, xdl, xuh, xul, dy, w, r, bt, skip_gain, init_state)
+    )(xdh, xdl, xuh, xul, dy, w, r, back, skip_gain, init_state)
     def after(m, token):
         return lax.optimization_barrier((m, token))[0]
 
-    near = mine[:3]
-    far = after(mine[3], local[2])
-    mine = [after(m, far) for m in near] + [far]
+    lead = after(mine[1], local[1])
+    mine = [lead if n == 1 else after(m, lead) for n, m in enumerate(mine)]
     theirs = [lax.ppermute(m, "ctx", swap).astype(f32) for m in mine]
     mine = [m.astype(f32) for m in mine]
 
@@ -453,7 +452,7 @@
             pltpu.VMEM((STATE, FEATS), f32),
         ],
         flops=1 << 30,
-    )(own, other, *mine, *theirs, xdh, xdl, xuh, xul, w, early, late, *local)
+    )(own, other, *mine, *theirs, xdh, xdl, xuh, xul, w, early, late, back, *local)
 
     moved = lax.all_to_all(rows, "head", split_axis=0, concat_axis=0, tiled=True)
     share = length // lax.axis_size("head")

time: 65.4 us -> 63.1 us (0.965)
  starting transfers between devices: 17.7 us -> 16.1 us
  Pallas kernels: 11.7 us -> 10.8 us
    ppermute x4, starting transfers between devices: 4.07 us -> 2.48 us  [per_device(): theirs = [lax.ppermute(m, 'ctx', swap).astype(f32) for m in mine]]
    pallas_call x1, Pallas kernels: 4.68 us -> 3.91 us  [per_device(): call(sums_kernel, (pltpu.VMEM((2 * STATE + 8, FEATS), f32), wide, wide, w...]
    ppermute x4, waiting for transfers between devices: 3.37 us -> 4.08 us  [per_device(): lax.ppermute(m.astype(jnp.float16), 'ctx', fan(hop))]
  transfers between devices with their start and end apart: 9 -> 9, of which waited for: 4 -> 5; matrix products, arithmetic and copies ran while one was open for 0% -> 0% of each run, Pallas kernels for 5% -> 5%
where the time goes in v4:
time: 63.1 us; the launch traced here: 63 us
  blocking collectives  28.5 us (45%)
  starting transfers between devices  16.1 us (26%)
  Pallas kernels  10.8 us (17%)
  waiting for transfers between devices  6.45 us (10%)
  between operations  0.94 us (1%)
    all_to_all x1, blocking collectives, per_device(): lax.all_to_all(rows, 'head', split_axis=0, concat_axis=0, tiled=True)  28.5 us
    ppermute x4, starting transfers between devices, per_device(): lax.ppermute(m.astype(jnp.float16), 'ctx', fan(hop))  10.3 us
    ppermute x4, waiting for transfers between devices, per_device(): lax.ppermute(m.astype(jnp.float16), 'ctx', fan(hop))  4.08 us
    pallas_call x1, Pallas kernels, per_device(): call(sums_kernel, (pltpu.VMEM((2 * STATE + 8, FEATS), f32), wide, wide, w...  3.91 us
    pallas_call x1, Pallas kernels, per_device(): call(local_kernel, (wide32, thin32, thin32, pltpu.VMEM((STATE, FEATS), f3...  3.36 us
    ppermute x1, starting transfers between devices, per_device(): other = lax.ppermute(own, 'ctx', swap)  3.32 us
    ppermute x4, starting transfers between devices, per_device(): theirs = [lax.ppermute(m, 'ctx', swap).astype(f32) for m in mine]  2.48 us
    pallas_call x1, Pallas kernels, per_device(): call(finish_kernel, jax.ShapeDtypeStruct((length, FEATS + 2 * STATE), bf1...  2.05 us
  transfers between devices with their start and end apart: 9, of which 5 were waited for; matrix products, arithmetic and copies ran while one was open for 0% of the time, Pallas kernels for 5%

profile of v4, /device:TPU:1, one launch (start us, length us, event | category | flops | bytes accessed | tf_op | source)
XLA Modules:
  0.0 63.0 jit_solution(11691532843028065185)
XLA Ops:
  0.6 3.9 %shard_map.103 = (f32[264,512]{1,0:T(8,128)S(1)}, bf16[1024,512]{1,0:T(8,128)(2,1)S(1)}, bf16[1024,512]{1,0:T(8,128)(2,1)S(1)}, bf16[1024,512]{1,0:T(8,128)(2,1)...) custom-call(bf16[1024,512]{1,0:T(8,128)(2,1)} %u_hbm.1, ...), custom_call_target="tpu_custom_call" | custom-call | flops 1073741824 | bytes 1048576 | tf_op jit(solution)/shard_map/pallas_call | solution.py:384
  4.5 0.0 copy-start
  4.6 0.0 copy-start.1
  4.6 3.3 %collective-permute-start = (f32[264,512]{1,0:T(8,128)S(1)}, f32[264,512]{1,0:T(8,128)S(1)}, u32[]{:S(2)}, u32[]{:S(2)}) collective-permute-start(f32[264,512]{1,0:T(8,128)S(1)} %get-tuple-element.26.own_ref), channel_id=1, source_target_pairs={{0,16},{16,0},{32,48},{48,32},{64,80},{80,64},{96,112},{112,96},{1... | collective-permute-start | bytes 1622024 | tf_op jit(solution)/shard_map/ppermute | solution.py:416
  7.9 1.6 %collective-permute-done.other_ref = f32[264,512]{1,0:T(8,128)S(1)} collective-permute-done((f32[264,512]{1,0:T(8,128)S(1)}, f32[264,512]{1,0:T(8,128)S(1)}, u32[]{:S(2)}, u32[]{:S(2)}) %collective-permute-start) | collective-permute-done | bytes 540704 | tf_op jit(solution)/shard_map/ppermute | solution.py:416
  9.5 0.3 shard_map.104
  9.7 4.4 %collective-permute-start.2 = (f16[136,512]{1,0:T(8,128)(2,1)S(1)}, f16[136,512]{1,0:T(8,128)(2,1)S(1)}, u32[]{:S(2)}, u32[]{:S(2)}) collective-permute-start(f16[136,512]{1,0:T(8,128)(2,1)S(1)} %convert_element_type.37), channel_id=1, source_target_pairs={{0,64},{32,96},{64,128},{96,160},{128,192},{160,224},{192,0},{224,... | collective-permute-start | bytes 417800 | tf_op jit(solution)/shard_map/ppermute | solution.py:426
  14.1 0.8 %collective-permute-start.3 = (f16[136,512]{1,0:T(8,128)(2,1)S(1)}, f16[136,512]{1,0:T(8,128)(2,1)S(1)}, u32[]{:S(2)}, u32[]{:S(2)}) collective-permute-start(f16[136,512]{1,0:T(8,128)(2,1)S(1)} %convert_element_type.40), channel_id=1, source_target_pairs={{0,96},{32,128},{64,160},{96,192},{128,224},{160,0},{192,32},{224,... | collective-permute-start | bytes 417800 | tf_op jit(solution)/shard_map/ppermute | solution.py:426
  14.9 0.6 collective-permute-start.1
  15.5 3.4 %shard_map.105 = (f32[1024,512]{1,0:T(8,128)S(1)}, f32[1024,128]{1,0:T(8,128)S(1)}, f32[1024,128]{1,0:T(8,128)S(1)}, f32[128,512]{1,0:T(8,128)S(1)}) custom-call(bf16[1024,512]{1,0:T(8,128)(2,1)S(1)} %get-tuple-element.29.xdh_ref, bf16[1024,512]{1,0:T(8,128)(2,1)S(1)} %get-tuple-element.30.xdl_ref, bf16[1024,512]{1,0:T(8,128)(2,1)S(1)} %get-tuple-element.31.xuh_ref, ...), custom_call_target="tpu_custom_call" | custom-call | bytes 1048576 | tf_op jit(solution)/shard_map/pallas_call | solution.py:430
  18.9 4.5 %collective-permute-start.4 = (f16[136,256]{1,0:T(8,128)(2,1)S(1)}, f16[136,256]{1,0:T(8,128)(2,1)S(1)}, u32[]{:S(2)}, u32[]{:S(2)}) collective-permute-start(f16[136,256]{1,0:T(8,128)(2,1)S(1)} %convert_element_type.42), channel_id=1, source_target_pairs={{0,128},{32,160},{64,192},{96,224},{128,0},{160,32},{192,64},{224,... | collective-permute-start | bytes 208904 | tf_op jit(solution)/shard_map/ppermute | solution.py:426
  23.5 0.0 collective-permute-done.2
  23.5 0.2 collective-permute-done.3
  23.6 0.3 collective-permute-done.1
  23.9 1.1 %collective-permute-start.5 = (f16[136,512]{1,0:T(8,128)(2,1)S(1)}, f16[136,512]{1,0:T(8,128)(2,1)S(1)}, u32[]{:S(2)}, u32[]{:S(2)}) collective-permute-start(f16[136,512]{1,0:T(8,128)(2,1)S(1)} %collective-permute-done.1), channel_id=1, source_target_pairs={{0,16},{16,0},{32,48},{48,32},{64,80},{80,64},{96,112},{112,96},{1... | collective-permute-start | bytes 417800 | tf_op jit(solution)/shard_map/ppermute | solution.py:441
  25.0 0.0 collective-permute-start.7
  25.0 0.5 collective-permute-start.6
  25.5 3.6 %collective-permute-done.4 = f16[136,256]{1,0:T(8,128)(2,1)S(1)} collective-permute-done((f16[136,256]{1,0:T(8,128)(2,1)S(1)}, f16[136,256]{1,0:T(8,128)(2,1)S(1)}, u32[]{:S(2)}, u32[]{:S(2)}) %collective-permute-start.4) | collective-permute-done | bytes 69664 | tf_op jit(solution)/shard_map/ppermute | solution.py:426
  29.1 0.9 %collective-permute-start.8 = (f16[136,256]{1,0:T(8,128)(2,1)S(1)}, f16[136,256]{1,0:T(8,128)(2,1)S(1)}, u32[]{:S(2)}, u32[]{:S(2)}) collective-permute-start(f16[136,256]{1,0:T(8,128)(2,1)S(1)} %collective-permute-done.4), channel_id=1, source_target_pairs={{0,16},{16,0},{32,48},{48,32},{64,80},{80,64},{96,112},{112,96},{1... | collective-permute-start | bytes 208904 | tf_op jit(solution)/shard_map/ppermute | solution.py:441
  30.1 0.8 %collective-permute-done.8 = f16[136,256]{1,0:T(8,128)(2,1)S(1)} collective-permute-done((f16[136,256]{1,0:T(8,128)(2,1)S(1)}, f16[136,256]{1,0:T(8,128)(2,1)S(1)}, u32[]{:S(2)}, u32[]{:S(2)}) %collective-permute-start.8) | collective-permute-done | bytes 69664 | tf_op jit(solution)/shard_map/ppermute | solution.py:441
  30.9 0.0 collective-permute-done.5
  31.1 2.1 %shard_map.106 = bf16[1024,768]{1,0:T(8,128)(2,1)S(1)} custom-call(f32[264,512]{1,0:T(8,128)S(1)} %get-tuple-element.26.own_ref, f32[264,512]{1,0:T(8,128)S(1)} %collective-permute-done.other_ref, f32[136,512]{1,0:T(8,128)S(1)} %convert_element_type.38.a_ref, f32[136,512]{1,0:T(8,128)S(1)} %convert_element_type.39.b_ref, ...), custom_call_target="tpu_custom_call" | custom-call | flops 1073741824 | bytes 1048576 | tf_op jit(solution)/shard_map/pallas_call | solution.py:444
  33.1 28.5 %all_to_all.11 = bf16[16,64,768]{2,1,0:T(8,128)(2,1)S(1)} all-to-all(bf16[16,64,768]{2,1,0:T(8,128)(2,1)S(1)} %bitcast.3), channel_id=1, replica_groups=mesh['ctx'=16,'head'=16] {'head'}, dimensions={0} | all-to-all | bytes 3145728 | tf_op jit(solution)/shard_map/all_to_all | solution.py:457
  61.7 1.2 %shard_map.107 = (bf16[64,8192]{1,0:T(8,128)(2,1)}, bf16[64,1024]{1,0:T(8,128)(2,1)}, bf16[64,1024]{1,0:T(8,128)(2,1)}) custom-call(bf16[1024,768]{1,0:T(8,128)(2,1)S(1)} %bitcast.4), custom_call_target="tpu_custom_call" | custom-call | bytes 1048576 | tf_op jit(solution)/shard_map/pallas_call | solution.py:459
  (16 shorter events, 0.2 us)
Async XLA Ops:
  4.5 11.0 %copy-start = (f32[8,64,128]{2,1,0:T(8,128)S(1)}, f32[8,64,128]{2,1,0:T(8,128)}, u32[]{:S(2)}) copy-start(f32[8,64,128]{2,1,0:T(8,128)} %init_ref.1) | copy-start | bytes 786436
  4.6 11.0 %copy-start.1 = (f32[8]{0:T(128)S(1)}, f32[8]{0:T(128)}, u32[]{:S(2)}) copy-start(f32[8]{0:T(128)} %skip_ref.1) | copy-start | bytes 100
  4.6 4.9 %collective-permute-start = (f32[264,512]{1,0:T(8,128)S(1)}, f32[264,512]{1,0:T(8,128)S(1)}, u32[]{:S(2)}, u32[]{:S(2)}) collective-permute-start(f32[264,512]{1,0:T(8,128)S(1)} %get-tuple-element.26.own_ref), channel_id=1, source_target_pairs={{0,16},{16,0},{32,48},{48,32},{64,80},{80,64},{96,112},{112,96},{1... | collective-permute-start | bytes 1622024 | tf_op jit(solution)/shard_map/ppermute | solution.py:416
  9.7 13.7 %collective-permute-start.2 = (f16[136,512]{1,0:T(8,128)(2,1)S(1)}, f16[136,512]{1,0:T(8,128)(2,1)S(1)}, u32[]{:S(2)}, u32[]{:S(2)}) collective-permute-start(f16[136,512]{1,0:T(8,128)(2,1)S(1)} %convert_element_type.37), channel_id=1, source_target_pairs={{0,64},{32,96},{64,128},{96,160},{128,192},{160,224},{192,0},{224,... | collective-permute-start | bytes 417800 | tf_op jit(solution)/shard_map/ppermute | solution.py:426
  14.1 9.5 %collective-permute-start.3 = (f16[136,512]{1,0:T(8,128)(2,1)S(1)}, f16[136,512]{1,0:T(8,128)(2,1)S(1)}, u32[]{:S(2)}, u32[]{:S(2)}) collective-permute-start(f16[136,512]{1,0:T(8,128)(2,1)S(1)} %convert_element_type.40), channel_id=1, source_target_pairs={{0,96},{32,128},{64,160},{96,192},{128,224},{160,0},{192,32},{224,... | collective-permute-start | bytes 417800 | tf_op jit(solution)/shard_map/ppermute | solution.py:426
  14.9 9.0 %collective-permute-start.1 = (f16[136,512]{1,0:T(8,128)(2,1)S(1)}, f16[136,512]{1,0:T(8,128)(2,1)S(1)}, u32[]{:S(2)}, u32[]{:S(2)}) collective-permute-start(f16[136,512]{1,0:T(8,128)(2,1)S(1)} %convert_element_type.36), channel_id=1, source_target_pairs={{0,32},{32,64},{64,96},{96,128},{128,160},{160,192},{192,224},{224... | collective-permute-start | bytes 417800 | tf_op jit(solution)/shard_map/ppermute | solution.py:426
  18.9 10.2 %collective-permute-start.4 = (f16[136,256]{1,0:T(8,128)(2,1)S(1)}, f16[136,256]{1,0:T(8,128)(2,1)S(1)}, u32[]{:S(2)}, u32[]{:S(2)}) collective-permute-start(f16[136,256]{1,0:T(8,128)(2,1)S(1)} %convert_element_type.42), channel_id=1, source_target_pairs={{0,128},{32,160},{64,192},{96,224},{128,0},{160,32},{192,64},{224,... | collective-permute-start | bytes 208904 | tf_op jit(solution)/shard_map/ppermute | solution.py:426
  23.9 7.0 %collective-permute-start.5 = (f16[136,512]{1,0:T(8,128)(2,1)S(1)}, f16[136,512]{1,0:T(8,128)(2,1)S(1)}, u32[]{:S(2)}, u32[]{:S(2)}) collective-permute-start(f16[136,512]{1,0:T(8,128)(2,1)S(1)} %collective-permute-done.1), channel_id=1, source_target_pairs={{0,16},{16,0},{32,48},{48,32},{64,80},{80,64},{96,112},{112,96},{1... | collective-permute-start | bytes 417800 | tf_op jit(solution)/shard_map/ppermute | solution.py:441
  25.0 6.0 %collective-permute-start.7 = (f16[136,512]{1,0:T(8,128)(2,1)S(1)}, f16[136,512]{1,0:T(8,128)(2,1)S(1)}, u32[]{:S(2)}, u32[]{:S(2)}) collective-permute-start(f16[136,512]{1,0:T(8,128)(2,1)S(1)} %collective-permute-done.3), channel_id=1, source_target_pairs={{0,16},{16,0},{32,48},{48,32},{64,80},{80,64},{96,112},{112,96},{1... | collective-permute-start | bytes 417800 | tf_op jit(solution)/shard_map/ppermute | solution.py:441
  25.0 6.0 %collective-permute-start.6 = (f16[136,512]{1,0:T(8,128)(2,1)S(1)}, f16[136,512]{1,0:T(8,128)(2,1)S(1)}, u32[]{:S(2)}, u32[]{:S(2)}) collective-permute-start(f16[136,512]{1,0:T(8,128)(2,1)S(1)} %collective-permute-done.2), channel_id=1, source_target_pairs={{0,16},{16,0},{32,48},{48,32},{64,80},{80,64},{96,112},{112,96},{1... | collective-permute-start | bytes 417800 | tf_op jit(solution)/shard_map/ppermute | solution.py:441
  29.1 1.8 %collective-permute-start.8 = (f16[136,256]{1,0:T(8,128)(2,1)S(1)}, f16[136,256]{1,0:T(8,128)(2,1)S(1)}, u32[]{:S(2)}, u32[]{:S(2)}) collective-permute-start(f16[136,256]{1,0:T(8,128)(2,1)S(1)} %collective-permute-done.4), channel_id=1, source_target_pairs={{0,16},{16,0},{32,48},{48,32},{64,80},{80,64},{96,112},{112,96},{1... | collective-permute-start | bytes 208904 | tf_op jit(solution)/shard_map/ppermute | solution.py:441

commit v5 on v4

--- a/solution.py
+++ b/solution.py
@@ -427,17 +427,16 @@
         for m, hop in zip(messages, (1, 2, 3, FAR))
     ]
 
+    def after(m, token):
+        return lax.optimization_barrier((m, token))[0]
+
     local = call(
         local_kernel,
         (wide32, thin32, thin32, pltpu.VMEM((STATE, FEATS), f32)),
         [IN_VMEM] * 8 + [IN_SMEM, IN_VMEM],
         flops=0,
-    )(xdh, xdl, xuh, xul, dy, w, r, back, skip_gain, init_state)
-    def after(m, token):
-        return lax.optimization_barrier((m, token))[0]
-
-    lead = after(mine[1], local[1])
-    mine = [lead if n == 1 else after(m, lead) for n, m in enumerate(mine)]
+    )(xdh, xdl, xuh, xul, dy, w, r, after(back, mine[0]), skip_gain, init_state)
+    mine = [mine[0]] + [after(m, local[1]) for m in mine[1:]]
     theirs = [lax.ppermute(m, "ctx", swap).astype(f32) for m in mine]
     mine = [m.astype(f32) for m in mine]
 

time: 63.1 us -> 62.8 us (level); the launches traced: 63 us -> 61.7 us
  starting transfers between devices: 16.1 us -> 15.1 us
    ppermute x4, starting transfers between devices: 2.48 us -> 1.49 us  [per_device(): theirs = [lax.ppermute(m, 'ctx', swap).astype(f32) for m in mine]]
  transfers between devices with their start and end apart: 9 -> 9, of which waited for: 5 -> 3; matrix products, arithmetic and copies ran while one was open for 0% -> 0% of each run, Pallas kernels for 5% -> 5%
where the time goes in v5:
time: 62.8 us; the launch traced here: 61.7 us
  blocking collectives  28.5 us (45%)
  starting transfers between devices  15.1 us (24%)
  Pallas kernels  10.8 us (17%)
  waiting for transfers between devices  6.14 us (10%)
  between operations  0.96 us (2%)
    all_to_all x1, blocking collectives, per_device(): lax.all_to_all(rows, 'head', split_axis=0, concat_axis=0, tiled=True)  28.5 us
    ppermute x4, starting transfers between devices, per_device(): lax.ppermute(m.astype(jnp.float16), 'ctx', fan(hop))  10.3 us
    pallas_call x1, Pallas kernels, per_device(): call(sums_kernel, (pltpu.VMEM((2 * STATE + 8, FEATS), f32), wide, wide, w...  3.91 us
    ppermute x4, waiting for transfers between devices, per_device(): lax.ppermute(m.astype(jnp.float16), 'ctx', fan(hop))  3.78 us
    pallas_call x1, Pallas kernels, per_device(): call(local_kernel, (wide32, thin32, thin32, pltpu.VMEM((STATE, FEATS), f3...  3.37 us
    ppermute x1, starting transfers between devices, per_device(): other = lax.ppermute(own, 'ctx', swap)  3.32 us
    pallas_call x1, Pallas kernels, per_device(): call(finish_kernel, jax.ShapeDtypeStruct((length, FEATS + 2 * STATE), bf1...  2.05 us
    ppermute x1, waiting for transfers between devices, per_device(): other = lax.ppermute(own, 'ctx', swap)  1.56 us
  transfers between devices with their start and end apart: 9, of which 3 were waited for; matrix products, arithmetic and copies ran while one was open for 0% of the time, Pallas kernels for 5%

profile of v5, /device:TPU:1, one launch (start us, length us, event | category | flops | bytes accessed | tf_op | source)
XLA Modules:
  0.0 61.7 jit_solution(4246098737656972479)
XLA Ops:
  0.6 3.9 %shard_map.103 = (f32[264,512]{1,0:T(8,128)S(1)}, bf16[1024,512]{1,0:T(8,128)(2,1)S(1)}, bf16[1024,512]{1,0:T(8,128)(2,1)S(1)}, bf16[1024,512]{1,0:T(8,128)(2,1)...) custom-call(bf16[1024,512]{1,0:T(8,128)(2,1)} %u_hbm.1, ...), custom_call_target="tpu_custom_call" | custom-call | flops 1073741824 | bytes 1048576 | tf_op jit(solution)/shard_map/pallas_call | solution.py:384
  4.5 0.0 copy-start
  4.6 0.0 copy-start.1
  4.6 3.3 %collective-permute-start = (f32[264,512]{1,0:T(8,128)S(1)}, f32[264,512]{1,0:T(8,128)S(1)}, u32[]{:S(2)}, u32[]{:S(2)}) collective-permute-start(f32[264,512]{1,0:T(8,128)S(1)} %get-tuple-element.26.own_ref), channel_id=1, source_target_pairs={{0,16},{16,0},{32,48},{48,32},{64,80},{80,64},{96,112},{112,96},{1... | collective-permute-start | bytes 1622024 | tf_op jit(solution)/shard_map/ppermute | solution.py:416
  7.9 1.6 %collective-permute-done.other_ref = f32[264,512]{1,0:T(8,128)S(1)} collective-permute-done((f32[264,512]{1,0:T(8,128)S(1)}, f32[264,512]{1,0:T(8,128)S(1)}, u32[]{:S(2)}, u32[]{:S(2)}) %collective-permute-start) | collective-permute-done | bytes 540704 | tf_op jit(solution)/shard_map/ppermute | solution.py:416
  9.5 0.3 shard_map.104
  9.7 3.9 %collective-permute-start.1 = (f16[136,512]{1,0:T(8,128)(2,1)S(1)}, f16[136,512]{1,0:T(8,128)(2,1)S(1)}, u32[]{:S(2)}, u32[]{:S(2)}) collective-permute-start(f16[136,512]{1,0:T(8,128)(2,1)S(1)} %convert_element_type.36), channel_id=1, source_target_pairs={{0,32},{32,64},{64,96},{96,128},{128,160},{160,192},{192,224},{224... | collective-permute-start | bytes 417800 | tf_op jit(solution)/shard_map/ppermute | solution.py:426
  13.7 1.7 %collective-permute-start.3 = (f16[136,512]{1,0:T(8,128)(2,1)S(1)}, f16[136,512]{1,0:T(8,128)(2,1)S(1)}, u32[]{:S(2)}, u32[]{:S(2)}) collective-permute-start(f16[136,512]{1,0:T(8,128)(2,1)S(1)} %convert_element_type.40), channel_id=1, source_target_pairs={{0,96},{32,128},{64,160},{96,192},{128,224},{160,0},{192,32},{224,... | collective-permute-start | bytes 417800 | tf_op jit(solution)/shard_map/ppermute | solution.py:426
  15.4 0.1 collective-permute-start.2
  15.5 4.5 %collective-permute-start.4 = (f16[136,256]{1,0:T(8,128)(2,1)S(1)}, f16[136,256]{1,0:T(8,128)(2,1)S(1)}, u32[]{:S(2)}, u32[]{:S(2)}) collective-permute-start(f16[136,256]{1,0:T(8,128)(2,1)S(1)} %convert_element_type.42), channel_id=1, source_target_pairs={{0,128},{32,160},{64,192},{96,224},{128,0},{160,32},{192,64},{224,... | collective-permute-start | bytes 208904 | tf_op jit(solution)/shard_map/ppermute | solution.py:426
  20.1 0.0 collective-permute-done.1
  20.1 3.4 %shard_map.105 = (f32[1024,512]{1,0:T(8,128)S(1)}, f32[1024,128]{1,0:T(8,128)S(1)}, f32[1024,128]{1,0:T(8,128)S(1)}, f32[128,512]{1,0:T(8,128)S(1)}) custom-call(bf16[1024,512]{1,0:T(8,128)(2,1)S(1)} %get-tuple-element.29.xdh_ref, bf16[1024,512]{1,0:T(8,128)(2,1)S(1)} %get-tuple-element.30.xdl_ref, bf16[1024,512]{1,0:T(8,128)(2,1)S(1)} %get-tuple-element.31.xuh_ref, ...), custom_call_target="tpu_custom_call" | custom-call | bytes 1048576 | tf_op jit(solution)/shard_map/pallas_call | solution.py:433
  23.5 0.0 collective-permute-done.3
  23.5 3.8 %collective-permute-done.2 = f16[136,512]{1,0:T(8,128)(2,1)S(1)} collective-permute-done((f16[136,512]{1,0:T(8,128)(2,1)S(1)}, f16[136,512]{1,0:T(8,128)(2,1)S(1)}, u32[]{:S(2)}, u32[]{:S(2)}) %collective-permute-start.2) | collective-permute-done | bytes 139296 | tf_op jit(solution)/shard_map/ppermute | solution.py:426
  27.2 0.0 collective-permute-start.5
  27.2 0.5 collective-permute-start.6
  27.7 0.0 collective-permute-start.7
  27.7 0.0 collective-permute-done.4
  27.8 1.0 %collective-permute-start.8 = (f16[136,256]{1,0:T(8,128)(2,1)S(1)}, f16[136,256]{1,0:T(8,128)(2,1)S(1)}, u32[]{:S(2)}, u32[]{:S(2)}) collective-permute-start(f16[136,256]{1,0:T(8,128)(2,1)S(1)} %collective-permute-done.4), channel_id=1, source_target_pairs={{0,16},{16,0},{32,48},{48,32},{64,80},{80,64},{96,112},{112,96},{1... | collective-permute-start | bytes 208904 | tf_op jit(solution)/shard_map/ppermute | solution.py:440
  28.8 0.8 %collective-permute-done.8 = f16[136,256]{1,0:T(8,128)(2,1)S(1)} collective-permute-done((f16[136,256]{1,0:T(8,128)(2,1)S(1)}, f16[136,256]{1,0:T(8,128)(2,1)S(1)}, u32[]{:S(2)}, u32[]{:S(2)}) %collective-permute-start.8) | collective-permute-done | bytes 69664 | tf_op jit(solution)/shard_map/ppermute | solution.py:440
  29.7 0.0 collective-permute-done.5
  29.8 2.1 %shard_map.106 = bf16[1024,768]{1,0:T(8,128)(2,1)S(1)} custom-call(f32[264,512]{1,0:T(8,128)S(1)} %get-tuple-element.26.own_ref, f32[264,512]{1,0:T(8,128)S(1)} %collective-permute-done.other_ref, f32[136,512]{1,0:T(8,128)S(1)} %convert_element_type.37.a_ref, f32[136,512]{1,0:T(8,128)S(1)} %convert_element_type.39.b_ref, ...), custom_call_target="tpu_custom_call" | custom-call | flops 1073741824 | bytes 1048576 | tf_op jit(solution)/shard_map/pallas_call | solution.py:443
  31.8 28.5 %all_to_all.11 = bf16[16,64,768]{2,1,0:T(8,128)(2,1)S(1)} all-to-all(bf16[16,64,768]{2,1,0:T(8,128)(2,1)S(1)} %bitcast.3), channel_id=1, replica_groups=mesh['ctx'=16,'head'=16] {'head'}, dimensions={0} | all-to-all | bytes 3145728 | tf_op jit(solution)/shard_map/all_to_all | solution.py:456
  60.4 1.2 %shard_map.107 = (bf16[64,8192]{1,0:T(8,128)(2,1)}, bf16[64,1024]{1,0:T(8,128)(2,1)}, bf16[64,1024]{1,0:T(8,128)(2,1)}) custom-call(bf16[1024,768]{1,0:T(8,128)(2,1)S(1)} %bitcast.4), custom_call_target="tpu_custom_call" | custom-call | bytes 1048576 | tf_op jit(solution)/shard_map/pallas_call | solution.py:458
  (16 shorter events, 0.2 us)
Async XLA Ops:
  4.5 15.5 %copy-start = (f32[8,64,128]{2,1,0:T(8,128)S(1)}, f32[8,64,128]{2,1,0:T(8,128)}, u32[]{:S(2)}) copy-start(f32[8,64,128]{2,1,0:T(8,128)} %init_ref.1) | copy-start | bytes 786436
  4.6 15.5 %copy-start.1 = (f32[8]{0:T(128)S(1)}, f32[8]{0:T(128)}, u32[]{:S(2)}) copy-start(f32[8]{0:T(128)} %skip_ref.1) | copy-start | bytes 100
  4.6 4.9 %collective-permute-start = (f32[264,512]{1,0:T(8,128)S(1)}, f32[264,512]{1,0:T(8,128)S(1)}, u32[]{:S(2)}, u32[]{:S(2)}) collective-permute-start(f32[264,512]{1,0:T(8,128)S(1)} %get-tuple-element.26.own_ref), channel_id=1, source_target_pairs={{0,16},{16,0},{32,48},{48,32},{64,80},{80,64},{96,112},{112,96},{1... | collective-permute-start | bytes 1622024 | tf_op jit(solution)/shard_map/ppermute | solution.py:416
  9.7 10.3 %collective-permute-start.1 = (f16[136,512]{1,0:T(8,128)(2,1)S(1)}, f16[136,512]{1,0:T(8,128)(2,1)S(1)}, u32[]{:S(2)}, u32[]{:S(2)}) collective-permute-start(f16[136,512]{1,0:T(8,128)(2,1)S(1)} %convert_element_type.36), channel_id=1, source_target_pairs={{0,32},{32,64},{64,96},{96,128},{128,160},{160,192},{192,224},{224... | collective-permute-start | bytes 417800 | tf_op jit(solution)/shard_map/ppermute | solution.py:426
  13.7 9.8 %collective-permute-start.3 = (f16[136,512]{1,0:T(8,128)(2,1)S(1)}, f16[136,512]{1,0:T(8,128)(2,1)S(1)}, u32[]{:S(2)}, u32[]{:S(2)}) collective-permute-start(f16[136,512]{1,0:T(8,128)(2,1)S(1)} %convert_element_type.40), channel_id=1, source_target_pairs={{0,96},{32,128},{64,160},{96,192},{128,224},{160,0},{192,32},{224,... | collective-permute-start | bytes 417800 | tf_op jit(solution)/shard_map/ppermute | solution.py:426
  15.4 11.8 %collective-permute-start.2 = (f16[136,512]{1,0:T(8,128)(2,1)S(1)}, f16[136,512]{1,0:T(8,128)(2,1)S(1)}, u32[]{:S(2)}, u32[]{:S(2)}) collective-permute-start(f16[136,512]{1,0:T(8,128)(2,1)S(1)} %convert_element_type.38), channel_id=1, source_target_pairs={{0,64},{32,96},{64,128},{96,160},{128,192},{160,224},{192,0},{224,... | collective-permute-start | bytes 417800 | tf_op jit(solution)/shard_map/ppermute | solution.py:426
  15.5 12.2 %collective-permute-start.4 = (f16[136,256]{1,0:T(8,128)(2,1)S(1)}, f16[136,256]{1,0:T(8,128)(2,1)S(1)}, u32[]{:S(2)}, u32[]{:S(2)}) collective-permute-start(f16[136,256]{1,0:T(8,128)(2,1)S(1)} %convert_element_type.42), channel_id=1, source_target_pairs={{0,128},{32,160},{64,192},{96,224},{128,0},{160,32},{192,64},{224,... | collective-permute-start | bytes 208904 | tf_op jit(solution)/shard_map/ppermute | solution.py:426
  27.2 2.4 %collective-permute-start.5 = (f16[136,512]{1,0:T(8,128)(2,1)S(1)}, f16[136,512]{1,0:T(8,128)(2,1)S(1)}, u32[]{:S(2)}, u32[]{:S(2)}) collective-permute-start(f16[136,512]{1,0:T(8,128)(2,1)S(1)} %collective-permute-done.1), channel_id=1, source_target_pairs={{0,16},{16,0},{32,48},{48,32},{64,80},{80,64},{96,112},{112,96},{1... | collective-permute-start | bytes 417800 | tf_op jit(solution)/shard_map/ppermute | solution.py:440
  27.2 2.5 %collective-permute-start.6 = (f16[136,512]{1,0:T(8,128)(2,1)S(1)}, f16[136,512]{1,0:T(8,128)(2,1)S(1)}, u32[]{:S(2)}, u32[]{:S(2)}) collective-permute-start(f16[136,512]{1,0:T(8,128)(2,1)S(1)} %collective-permute-done.2), channel_id=1, source_target_pairs={{0,16},{16,0},{32,48},{48,32},{64,80},{80,64},{96,112},{112,96},{1... | collective-permute-start | bytes 417800 | tf_op jit(solution)/shard_map/ppermute | solution.py:440
  27.7 2.0 %collective-permute-start.7 = (f16[136,512]{1,0:T(8,128)(2,1)S(1)}, f16[136,512]{1,0:T(8,128)(2,1)S(1)}, u32[]{:S(2)}, u32[]{:S(2)}) collective-permute-start(f16[136,512]{1,0:T(8,128)(2,1)S(1)} %collective-permute-done.3), channel_id=1, source_target_pairs={{0,16},{16,0},{32,48},{48,32},{64,80},{80,64},{96,112},{112,96},{1... | collective-permute-start | bytes 417800 | tf_op jit(solution)/shard_map/ppermute | solution.py:440
  27.8 1.9 %collective-permute-start.8 = (f16[136,256]{1,0:T(8,128)(2,1)S(1)}, f16[136,256]{1,0:T(8,128)(2,1)S(1)}, u32[]{:S(2)}, u32[]{:S(2)}) collective-permute-start(f16[136,256]{1,0:T(8,128)(2,1)S(1)} %collective-permute-done.4), channel_id=1, source_target_pairs={{0,16},{16,0},{32,48},{48,32},{64,80},{80,64},{96,112},{112,96},{1... | collective-permute-start | bytes 208904 | tf_op jit(solution)/shard_map/ppermute | solution.py:440
